TPU v7x, 256 devices: a whole 4x4x8 slice. The times are simulated.
256 devices in a mesh: dp: 2 (over z_hi), seq: 64 (over z_lo, x, y), head: 2 (over core).
Axes of the slice: x: 4, y: 4, z: 8 (z_hi: 2, z_lo: 4; z = z_hi * 4 + z_lo), core: 2. Of those that a mesh axis runs over, the one named last changes fastest.
Arguments:
- fine_queries: bfloat16 [2, 24576, 32, 128], P('dp', 'seq', 'head'), may hold values from -96 to 96
- fine_keys: bfloat16 [2, 24576, 32, 128], P('dp', 'seq', 'head'), may hold values from -10 to 10
- fine_values: bfloat16 [2, 24576, 32, 128], P('dp', 'seq', 'head'), may hold values from -6 to 6
- coarse_keys: bfloat16 [2, 256, 32, 128], P('dp', 'seq', 'head'), may hold values from -8 to 8
- coarse_values: bfloat16 [2, 256, 32, 128], P('dp', 'seq', 'head'), may hold values from -6 to 6
- out_grad: bfloat16 [2, 24576, 32, 128], P('dp', 'seq', 'head'), may hold values from -6 to 6
Outputs:
- attended: bfloat16 [2, 24576, 32, 128], P('dp', 'seq', 'head')
- query_grad: bfloat16 [2, 24576, 32, 128], P('dp', 'seq', 'head')
- key_grad: bfloat16 [2, 24576, 32, 128], P('dp', 'seq', 'head')
- value_grad: bfloat16 [2, 24576, 32, 128], P('dp', 'seq', 'head')
All inputs are finite; a program needn't handle non-finite values.
Results may differ from a plain program's by a relative error of at most 0.012.
Values may be sent and summed in bfloat16 or wider, within the bound.
No kernel may reach another device: no remote copies, remote signals or barrier semaphores. Data moves between devices by JAX's collectives and lax.ppermute only.
A program may use at most 128 MiB of HBM per device.

v0:
```python
import functools

import jax
import jax.numpy as jnp
from jax import lax
from jax.experimental import pallas as pl
from jax.experimental.pallas import tpu as pltpu
from jax.sharding import PartitionSpec as P

TILE_H = 24
TILE_W = 16
RADIUS = 4
TILES_X = 8
TOKENS = TILE_H * TILE_W
EDGE = RADIUS * TILE_W
SIDE = TILE_H * RADIUS
CORNER = RADIUS * RADIUS
STRIP = SIDE + 2 * CORNER
CHUNKS = 2
BLOCK_ROWS = 8
BLOCKS = TILE_H // BLOCK_ROWS
QUERIES = BLOCK_ROWS * TILE_W
WIN_ROWS = BLOCK_ROWS + 2 * RADIUS
NEAR = WIN_ROWS * (TILE_W + 2 * RADIUS)
FLOOR = -1e30
LOG2E = 1.4426950408889634
BF = jnp.bfloat16
F32 = jnp.float32
SMEM = pl.BlockSpec(memory_space=pltpu.SMEM)
VMEM = pl.BlockSpec(memory_space=pltpu.VMEM)
PARAMS = pltpu.CompilerParams(vmem_limit_bytes=62 << 20)


def nt(a, b):
    return lax.dot_general(a, b, (((1,), (1,)), ((), ())), preferred_element_type=F32)


def tn(a, b):
    return lax.dot_general(a, b, (((0,), (0,)), ((), ())), preferred_element_type=F32)


def nn(a, b):
    return lax.dot_general(a, b, (((1,), (0,)), ((), ())), preferred_element_type=F32)


def sds(*shape):
    return jax.ShapeDtypeStruct(shape, BF)


def exchange(value, rows, which):
    count = lax.axis_size("seq")
    pairs = []
    for source in range(count):
        row, col = divmod(source, TILES_X)
        place, extent = (row, count // TILES_X) if rows else (col, TILES_X)
        target = ((place + which) ^ 1) - which
        if not 0 <= target < extent:
            target = place
        pairs.append((source, target * TILES_X + col if rows else row * TILES_X + target))
    return lax.ppermute(value, "seq", pairs)


def widened(block, stride):
    count = lax.axis_size("seq")

    def swapped(mask):
        pairs = [(source, source ^ (mask * stride)) for source in range(count)]
        return lax.ppermute(block, "seq", pairs)

    return [block] + [swapped(mask) for mask in (1, 2, 3)]


def pairs_to_heads_kernel(k, v, kv):
    for i, x in enumerate((k, v)):
        kv[:, i] = jnp.swapaxes(x[0], 0, 1)


def pairs_to_heads(k, v):
    t, h, d = k.shape[1:]
    return pl.pallas_call(
        pairs_to_heads_kernel, out_shape=sds(h, 2, t, d), compiler_params=PARAMS, name="pairs_to_heads"
    )(k, v)


def to_heads_kernel(x, y, a, b):
    a[...] = jnp.swapaxes(x[0], 0, 1)
    b[...] = jnp.swapaxes(y[0], 0, 1)


def to_heads(x, y):
    t, h, d = x.shape[1:]
    return pl.pallas_call(
        to_heads_kernel, out_shape=[sds(h, t, d)] * 2, compiler_params=PARAMS, name="to_heads"
    )(x, y)


def halo_to_heads_kernel(even, x, y, up, dn):
    for i in range(2):
        a = jnp.swapaxes(x[:, i], 0, 1)
        b = jnp.swapaxes(y[:, i], 0, 1)
        up[:, i] = lax.select(even[0] == 1, b, a)
        dn[:, i] = lax.select(even[0] == 1, a, b)


def halo_to_heads(even, x, y):
    t, _, h, d = x.shape
    return pl.pallas_call(
        halo_to_heads_kernel,
        in_specs=[SMEM, VMEM, VMEM],
        out_shape=[sds(h, 2, t, d)] * 2,
        compiler_params=PARAMS,
        name="halo_to_heads",
    )(even, x, y)


def far_kernel(*refs):
    out = refs[-1]
    n = refs[0].shape[0]
    for j, piece in enumerate(refs[:-1]):
        for i in range(2):
            out[:, i, j * n : (j + 1) * n] = jnp.swapaxes(piece[:, i], 0, 1)


def far_heads(pieces):
    n, _, h, d = pieces[0].shape
    return pl.pallas_call(
        far_kernel, out_shape=sds(h, 2, n * len(pieces), d), compiler_params=PARAMS, name="far_heads"
    )(*pieces)


def columns_kernel(even, ka, kb, va, vb, *outs):
    h, d = ka.shape[2:]
    n = h // CHUNKS
    for j, mine in enumerate(((ka, va), (kb, vb))):
        for i in range(2):
            x = mine[i][...].reshape(SIDE, h, d)
            for c in range(CHUNKS):
                outs[j * CHUNKS + c][CORNER : CORNER + SIDE, i] = x[:, c * n : (c + 1) * n]


def columns(even, k, v):
    h, d = k.shape[1:]
    k = k.reshape(TILE_H, TILE_W, h, d)
    v = v.reshape(TILE_H, TILE_W, h, d)
    block = (TILE_H, RADIUS, h, d)
    last = TILE_W // RADIUS - 1
    side_a = pl.BlockSpec(block, lambda g, e: (0, last * e[1], 0, 0))
    side_b = pl.BlockSpec(block, lambda g, e: (0, last * (1 - e[1]), 0, 0))
    shape = (STRIP, 2, h // CHUNKS, d)
    return pl.pallas_call(
        columns_kernel,
        grid_spec=pltpu.PrefetchScalarGridSpec(
            num_scalar_prefetch=1,
            grid=(1,),
            in_specs=[side_a, side_b, side_a, side_b],
            out_specs=[pl.BlockSpec(shape, lambda g, e: (0, 0, 0, 0))] * (2 * CHUNKS),
        ),
        out_shape=[sds(*shape)] * (2 * CHUNKS),
        compiler_params=PARAMS,
        name="columns",
    )(even, k, k, v, v)


def corners_kernel(even, a, b, *refs):
    outs = refs[len(refs) // 2 :]
    h = a.shape[2]
    n = h // CHUNKS
    for g, rows in enumerate((a, b)):

        @pl.when(pl.program_id(0) == g)
        def _():
            for j, e in enumerate((even[1], 1 - even[1])):
                for r in range(RADIUS):
                    start = r * TILE_W + (TILE_W - RADIUS) * e
                    for i in range(2):
                        x = rows[pl.ds(start, RADIUS), i]
                        for c in range(CHUNKS):
                            out = outs[j * CHUNKS + c]
                            out[r * RADIUS : (r + 1) * RADIUS, i] = x[:, c * n : (c + 1) * n]


def corners(even, a, b, strips):
    whole = pl.BlockSpec(a.shape, lambda g, e: (0, 0, 0, 0))
    last = STRIP // CORNER - 1
    end = pl.BlockSpec((CORNER,) + strips[0].shape[1:], lambda g, e: (last * (g ^ e[0]), 0, 0, 0))
    outs = pl.pallas_call(
        corners_kernel,
        grid_spec=pltpu.PrefetchScalarGridSpec(
            num_scalar_prefetch=1,
            grid=(2,),
            in_specs=[whole, whole] + [pl.BlockSpec(memory_space=pl.ANY)] * len(strips),
            out_specs=[end] * len(strips),
        ),
        out_shape=[sds(*x.shape) for x in strips],
        input_output_aliases={3 + i: i for i in range(len(strips))},
        compiler_params=PARAMS,
        name="corners",
    )(even, a, b, *strips)
    return outs[:CHUNKS], outs[CHUNKS:]


def to_tokens_kernel(*refs):
    n = (len(refs) - 2) // 2
    for j in range(2):
        x = jnp.concatenate([r[...] for r in refs[j * n : (j + 1) * n]], 0)
        refs[2 * n + j][0] = jnp.swapaxes(x, 0, 1)


def to_tokens(xs, ys):
    h, t, d = xs[0].shape
    return pl.pallas_call(
        to_tokens_kernel,
        out_shape=[sds(1, t, h * len(xs), d)] * 2,
        compiler_params=PARAMS,
        name="to_tokens",
    )(*xs, *ys)


def fold_kernel(even, gup, gdn, from_a, from_b, a, b):
    h, _, t, d = gup.shape
    for i in range(2):
        folded = []
        for g, o in ((gup, 0), (gdn, STRIP - CORNER)):
            x = jnp.swapaxes(g[:, i], 0, 1).astype(F32).reshape(RADIUS, TILE_W, h, d)
            sa, sb = (
                jnp.swapaxes(s[:, i, o : o + CORNER], 0, 1).astype(F32).reshape(RADIUS, RADIUS, h, d)
                for s in (from_a, from_b)
            )
            left = lax.select(even[1] == 1, sb, sa)
            right = lax.select(even[1] == 1, sa, sb)
            x = jnp.concatenate(
                [x[:, :RADIUS] + left, x[:, RADIUS : TILE_W - RADIUS], x[:, TILE_W - RADIUS :] + right], 1
            )
            folded.append(x.reshape(t, h, d).astype(BF))
        a[:, i] = lax.select(even[0] == 1, folded[1], folded[0])
        b[:, i] = lax.select(even[0] == 1, folded[0], folded[1])


def fold(even, gup, gdn, from_a, from_b):
    h, _, t, d = gup.shape
    return pl.pallas_call(
        fold_kernel,
        in_specs=[SMEM] + [VMEM] * 4,
        out_shape=[sds(t, 2, h, d)] * 2,
        compiler_params=PARAMS,
        name="fold",
    )(even, gup, gdn, from_a, from_b)


def premerge_kernel(even, *refs):
    own, from_a, from_b = (refs[c * CHUNKS : (c + 1) * CHUNKS] for c in range(3))
    for i, out in enumerate(refs[3 * CHUNKS :]):
        h, d = out.shape[2:]

        def tokens(parts, rows, *lead):
            x = jnp.concatenate([r[:, i, rows] for r in parts], 0)
            return jnp.swapaxes(x, 0, 1).astype(F32).reshape(*lead, h, d)

        t = tokens(own, slice(0, TOKENS), TILE_H, TILE_W)
        sa = tokens(from_a, slice(CORNER, CORNER + SIDE), TILE_H, RADIUS)
        sb = tokens(from_b, slice(CORNER, CORNER + SIDE), TILE_H, RADIUS)
        le = lax.select(even[1] == 1, sb, sa)
        ri = lax.select(even[1] == 1, sa, sb)
        t = jnp.concatenate(
            [t[:, :RADIUS] + le, t[:, RADIUS : TILE_W - RADIUS], t[:, TILE_W - RADIUS :] + ri], 1
        )
        out[0] = t.reshape(TOKENS, h, d).astype(BF)


def premerge(even, own, from_a, from_b):
    h, _, t, d = own[0].shape
    return pl.pallas_call(
        premerge_kernel,
        in_specs=[SMEM] + [VMEM] * (3 * CHUNKS),
        out_shape=[sds(1, t, h * CHUNKS, d)] * 2,
        compiler_params=PARAMS,
        name="premerge",
    )(even, *own, *from_a, *from_b)


def finish_kernel(even, *refs):
    sums = refs[:2]
    parts = [refs[2 + c * CHUNKS : 2 + (c + 1) * CHUNKS] for c in range(2)]
    outs = refs[2 + 2 * CHUNKS :]
    for g in range(2):

        @pl.when(pl.program_id(0) == g)
        def _():
            for i in range(2):
                x = jnp.concatenate([r[:, i] for r in parts[g]], 1).astype(F32)
                outs[i][0] = (sums[i][0].astype(F32) + x).astype(BF)


def finish(even, dk, dv, from_a, from_b):
    h, d = dk.shape[2:]
    last = TOKENS // EDGE - 1
    rows = pl.BlockSpec((1, EDGE, h, d), lambda g, e: (0, last * (g ^ e[0]), 0, 0))
    part = pl.BlockSpec(from_a[0].shape, lambda g, e: (0, 0, 0, 0))
    return pl.pallas_call(
        finish_kernel,
        grid_spec=pltpu.PrefetchScalarGridSpec(
            num_scalar_prefetch=1,
            grid=(2,),
            in_specs=[rows, rows] + [part] * (2 * CHUNKS),
            out_specs=[rows, rows],
        ),
        out_shape=[sds(*dk.shape)] * 2,
        input_output_aliases={1: 0, 2: 1},
        compiler_params=PARAMS,
        name="finish",
    )(even, dk, dv, *from_a, *from_b)


def attend_kernel(
    heads, q, do, kv, up, dn, far, sa, sb, bias, even, att, dq, own, gup, gdn, ga, gb, strips_lr
):
    @pl.when(pl.program_id(0) == 0)
    def _():
        for src, side in ((sa, even[1]), (sb, 1 - even[1])):
            for i in range(2):
                strips_lr[side, :, i] = jnp.swapaxes(src[:, i], 0, 1)

    first = pl.program_id(0) * heads
    scale = q.shape[-1] ** -0.5
    half = WIN_ROWS * RADIUS
    mid = WIN_ROWS * TILE_W

    def strips(h, i):
        center = jnp.concatenate([up[h, i], kv[h, i], dn[h, i]], 0)
        return center, strips_lr[0, first + h, i], strips_lr[1, first + h, i], far[h, i]

    def window(parts, b):
        c, l, r, f = parts
        o, s = b * BLOCK_ROWS * TILE_W, b * BLOCK_ROWS * RADIUS
        return jnp.concatenate([c[o : o + mid], l[s : s + half], r[s : s + half], f], 0)

    parts = [[strips(h, i) for i in range(2)] for h in range(heads)]
    grads = {}

    def block(h, b):
        rows = slice(b * QUERIES, (b + 1) * QUERIES)
        queries, cots = q[h, rows], do[h, rows]
        keys, values = window(parts[h][0], b), window(parts[h][1], b)
        s = nt(queries, keys)
        dp = nt(cots, values)
        yield
        s = s * (scale * LOG2E)
        s = jnp.concatenate([s[:, :NEAR] + bias[b], s[:, NEAR:]], 1)
        top = jnp.max(s, 1, keepdims=True)
        yield
        e = jnp.exp2(s - top)
        inverse = 1.0 / jnp.sum(e, 1, keepdims=True)
        yield
        p = e * inverse
        rounded = p.astype(BF)
        out = nn(rounded, values).astype(BF)
        dv = tn(rounded[:, :NEAR], cots)
        yield
        att[h, rows] = out
        delta = jnp.sum(out.astype(F32) * cots.astype(F32), 1, keepdims=True)
        ds = (p * (dp - delta) * scale).astype(BF)
        dqs = nn(ds, keys)
        dk = tn(ds[:, :NEAR], queries)
        yield
        dq[h, rows] = dqs.astype(BF)
        grads[h, b] = (dk, dv)

    live = [block(h, b) for h in range(heads) for b in range(BLOCKS)]
    while live:
        for g in list(live):
            try:
                next(g)
            except StopIteration:
                live.remove(g)

    step = BLOCK_ROWS * TILE_W
    for h in range(heads):
        for i in range(2):
            g = [grads[h, b][i] for b in range(BLOCKS)]
            c = [g[0][:step], g[0][step:mid] + g[1][:step], g[1][step:mid] + g[2][:step], g[2][step:mid]]
            c = jnp.concatenate(c, 0)
            gup[h, i] = c[:EDGE].astype(BF)
            own[h, i] = c[EDGE : EDGE + TOKENS].astype(own.dtype)
            gdn[h, i] = c[EDGE + TOKENS :].astype(BF)
            w = BLOCK_ROWS * RADIUS
            sides = []
            for j in range(2):
                s = [x[mid + j * half : mid + (j + 1) * half] for x in g]
                s = jnp.concatenate([s[0][:w], s[0][w:] + s[1][:w], s[1][w:] + s[2][:w], s[2][w:]], 0)
                sides.append(s.astype(BF))
            ga[h, i] = lax.select(even[1] == 1, sides[1], sides[0])
            gb[h, i] = lax.select(even[1] == 1, sides[0], sides[1])


def attend(chunk, even, q, do, kv, up, dn, far, sa, sb, bias, heads=2):
    _, t, d = q.shape
    h = sa.shape[2]
    steps = h // heads

    def spec(x, offset=0):
        return pl.BlockSpec((heads,) + x.shape[1:], lambda g: (g + offset,) + (0,) * (len(x.shape) - 1))

    def whole(x):
        return pl.BlockSpec(x.shape, lambda g: (0,) * len(x.shape))

    outs = [sds(h, t, d)] * 2 + [sds(h, 2, n, d) for n in (t, EDGE, EDGE, STRIP, STRIP)]
    flops = h * BLOCKS * QUERIES * (4 * (NEAR + far.shape[2]) + 2 * NEAR) * d * 2
    args = (q, do, kv, up, dn, far)
    return pl.pallas_call(
        functools.partial(attend_kernel, heads),
        grid=(steps,),
        in_specs=[spec(x, chunk * steps) for x in args] + [whole(x) for x in (sa, sb, bias)] + [SMEM],
        out_specs=[spec(x) for x in outs],
        out_shape=outs,
        scratch_shapes=[pltpu.VMEM((2, h, 2, STRIP, d), BF)],
        compiler_params=PARAMS,
        cost_estimate=pl.CostEstimate(flops=flops, bytes_accessed=12 << 20, transcendentals=0),
        name="attend",
    )(*args, sa, sb, bias, even)


def near_bias():
    position = lax.axis_index("seq")
    tiles_y = lax.axis_size("seq") // TILES_X
    shape = (BLOCKS, QUERIES, NEAR)
    b = lax.broadcasted_iota(jnp.int32, shape, 0)
    i = lax.broadcasted_iota(jnp.int32, shape, 1)
    k = lax.broadcasted_iota(jnp.int32, shape, 2)
    mid = WIN_ROWS * TILE_W
    half = WIN_ROWS * RADIUS
    k_row = jnp.where(k < mid, k // TILE_W, (k - mid) % half // RADIUS) - RADIUS
    side = jnp.where(k < mid + half, k % RADIUS - RADIUS, k % RADIUS + TILE_W)
    k_col = jnp.where(k < mid, k % TILE_W, side)
    seen = (jnp.abs(k_row - i // TILE_W) <= RADIUS) & (jnp.abs(k_col - i % TILE_W) <= RADIUS)
    row = position // TILES_X * TILE_H + b * BLOCK_ROWS + k_row
    col = position % TILES_X * TILE_W + k_col
    inside = (row >= 0) & (row < tiles_y * TILE_H) & (col >= 0) & (col < TILES_X * TILE_W)
    return jnp.where(seen & inside, 0.0, FLOOR).astype(F32)


def shards(fine_queries, fine_keys, fine_values, coarse_keys, coarse_values, out_grad):
    position = lax.axis_index("seq")
    even = jnp.stack([1 - position // TILES_X % 2, 1 - position % TILES_X % 2]).astype(jnp.int32)
    coarse = jnp.concatenate(widened(jnp.stack([coarse_keys[0], coarse_values[0]], 1), 4), 0)
    start = even[0] * (TOKENS - EDGE)
    rows = [
        jnp.stack([lax.dynamic_slice_in_dim(x[0], o, EDGE, 0) for x in (fine_keys, fine_values)], 1)
        for o in (start, TOKENS - EDGE - start)
    ]
    coarse, *rows = lax.optimization_barrier((coarse, *rows))
    row_a, row_b = (exchange(x, True, which) for which, x in enumerate(rows))
    coarse = jnp.concatenate(widened(coarse, 16), 0)
    coarse, fine_queries, out_grad, fine_keys, fine_values = lax.optimization_barrier(
        (coarse, fine_queries, out_grad, fine_keys, fine_values)
    )
    pieces = widened(coarse, 1)
    strips = columns(even, fine_keys[0], fine_values[0])
    queries, cots = to_heads(fine_queries, out_grad)
    kv = pairs_to_heads(fine_keys, fine_values)
    row_a, row_b, kv, queries, cots, *strips = lax.optimization_barrier(
        (row_a, row_b, kv, queries, cots, *strips)
    )
    sides = corners(even, row_a, row_b, strips)
    side_a, side_b = ([exchange(x, False, which) for x in xs] for which, xs in enumerate(sides))
    up, dn = halo_to_heads(even, row_a, row_b)
    far = far_heads(pieces)
    bias = near_bias()
    att, dq, own, to_a, to_b, from_a, from_b = ([] for _ in range(7))
    for c in range(CHUNKS):
        a, b, mine, gup, gdn, ga, gb = attend(
            c, even, queries, cots, kv, up, dn, far, side_a[c], side_b[c], bias
        )
        from_a.append(exchange(ga, False, 0))
        from_b.append(exchange(gb, False, 1))
        att.append(a)
        dq.append(b)
        own.append(mine)
        ra, rb = fold(even, gup, gdn, from_a[c], from_b[c])
        to_a.append(exchange(ra, True, 0))
        to_b.append(exchange(rb, True, 1))
    attended, query_grad = to_tokens(att, dq)
    dk, dv = premerge(even, own, from_a, from_b)
    key_grad, value_grad = finish(even, dk, dv, to_a, to_b)
    return (attended, query_grad, key_grad, value_grad)


def solution(mesh):
    spec = P("dp", "seq", "head", None)
    return jax.shard_map(
        shards, mesh=mesh, in_specs=(spec,) * 6, out_specs=(spec,) * 4, check_vma=False
    )
```

profile of v0, /device:TPU:6, one launch (start us, length us, event | category | flops | bytes accessed | tf_op | source)
XLA Modules:
  0.0 144.1 jit_solution(9637905097130705986)
XLA Ops:
  0.6 0.7 pad_maximum_fusion.4
  1.4 2.2 %collective-permute-start.2 = (bf16[4,2,16,128]{3,2,1,0:T(8,128)(2,1)S(1)}, bf16[4,2,16,128]{3,2,1,0:T(8,128)(2,1)S(1)}, u32[]{:S(2)}, u32[]{:S(2)}) collective-permute-start(bf16[4,2,16,128]{3,2,1,0:T(8,128)(2,1)S(1)} %pad_maximum_fusion.4), channel_id=1, source_target_pairs={{0,24},{2,26},{4,28},{6,30},{8,16},{10,18},{12,20},{14,22},{16,8},... | collective-permute-start | bytes 98312 | tf_op jit(solution)/shard_map/ppermute | solution.py:68
  3.6 0.7 collective-permute-start.1
  4.3 1.2 collective-permute-start
  5.5 1.4 dynamic-slice_bitcast_fusion
  6.9 0.0 copy-start.12
  6.9 0.0 copy-start.13
  6.9 0.8 pad_maximum_fusion.1
  7.7 0.8 pad_maximum_fusion
  8.6 0.0 collective-permute-done.2
  8.6 0.4 collective-permute-done.1
  9.0 4.3 %collective-permute-start.7 = (bf16[16,2,16,128]{3,2,1,0:T(8,128)(2,1)S(1)}, bf16[16,2,16,128]{3,2,1,0:T(8,128)(2,1)S(1)}, u32[]{:S(2)}, u32[]{:S(2)}) collective-permute-start(bf16[16,2,16,128]{3,2,1,0:T(8,128)(2,1)S(1)} %pad_maximum_fusion.3), channel_id=1, source_target_pairs={{0,96},{2,98},{4,100},{6,102},{8,104},{10,106},{12,108},{14,110},{... | collective-permute-start | bytes 393224 | tf_op jit(solution)/shard_map/ppermute | solution.py:68
  13.4 0.0 collective-permute-start.6
  13.4 0.7 collective-permute-start.5
  14.1 1.5 %collective-permute-start.3 = (bf16[64,2,16,128]{3,2,1,0:T(8,128)(2,1)}, bf16[64,2,16,128]{3,2,1,0:T(8,128)(2,1)S(1)}, u32[]{:S(2)}, u32[]{:S(2)}) collective-permute-start(bf16[64,2,16,128]{3,2,1,0:T(8,128)(2,1)} %pad_maximum_fusion), channel_id=1, source_target_pairs={{0,16},{2,18},{4,20},{6,22},{8,24},{10,26},{12,28},{14,30},{16,0},... | collective-permute-start | bytes 1572872 | tf_op jit(solution)/shard_map/ppermute | solution.py:60
  15.5 4.7 %collective-permute-start.4 = (bf16[64,2,16,128]{3,2,1,0:T(8,128)(2,1)}, bf16[64,2,16,128]{3,2,1,0:T(8,128)(2,1)S(1)}, u32[]{:S(2)}, u32[]{:S(2)}) collective-permute-start(bf16[64,2,16,128]{3,2,1,0:T(8,128)(2,1)} %pad_maximum_fusion.1), channel_id=1, source_target_pairs={{0,0},{2,2},{4,4},{6,6},{8,8},{10,10},{12,12},{14,14},{16,32},{18,... | collective-permute-start | bytes 1572872 | tf_op jit(solution)/shard_map/ppermute | solution.py:60
  20.3 0.0 collective-permute-done.7
  20.3 2.8 %collective-permute-done.6 = bf16[16,2,16,128]{3,2,1,0:T(8,128)(2,1)S(1)} collective-permute-done((bf16[16,2,16,128]{3,2,1,0:T(8,128)(2,1)S(1)}, bf16[16,2,16,128]{3,2,1,0:T(8,128)(2,1)S(1)}, u32[]{:S(2)}, u32[]{:S(2)}) %collective-permute-start.6) | collective-permute-done | bytes 131104 | tf_op jit(solution)/shard_map/ppermute | solution.py:68
  23.1 0.0 collective-permute-done.5
  23.1 0.1 pad_maximum_fusion.2.refs_0_
  23.2 3.1 %collective-permute-start.10 = (bf16[64,2,16,128]{3,2,1,0:T(8,128)(2,1)S(1)}, bf16[64,2,16,128]{3,2,1,0:T(8,128)(2,1)}, u32[]{:S(2)}, u32[]{:S(2)}) collective-permute-start(bf16[64,2,16,128]{3,2,1,0:T(8,128)(2,1)S(1)} %pad_maximum_fusion.2.refs_0_), channel_id=1, source_target_pairs={{0,6},{2,4},{4,2},{6,0},{8,14},{10,12},{12,10},{14,8},{16,22},{18,... | collective-permute-start | bytes 1572872 | tf_op jit(solution)/shard_map/ppermute | solution.py:68
  26.3 0.6 collective-permute-start.9
  26.9 0.7 pad_add_fusion.even
  27.6 0.5 collective-permute-start.8
  28.1 4.7 %pairs_to_heads.1.kv = bf16[16,2,384,128]{3,2,1,0:T(8,128)(2,1)} custom-call(bf16[1,384,16,128]{3,2,1,0:T(8,128)(2,1)} %k, bf16[1,384,16,128]{3,2,1,0:T(8,128)(2,1)} %v), custom_call_target="tpu_custom_call" | custom-call | tf_op jit(solution)/shard_map/pairs_to_heads/pallas_call | solution.py:80
  32.8 4.2 %to_heads.1 = (bf16[16,384,128]{2,1,0:T(8,128)(2,1)}, bf16[16,384,128]{2,1,0:T(8,128)(2,1)}) custom-call(bf16[1,384,16,128]{3,2,1,0:T(8,128)(2,1)} %x, bf16[1,384,16,128]{3,2,1,0:T(8,128)(2,1)} %y), custom_call_target="tpu_custom_call" | custom-call | tf_op jit(solution)/shard_map/to_heads/pallas_call | solution.py:92
  37.1 3.6 %columns.1 = (bf16[128,2,8,128]{3,2,1,0:T(8,128)(2,1)}, bf16[128,2,8,128]{3,2,1,0:T(8,128)(2,1)}, bf16[128,2,8,128]{3,2,1,0:T(8,128)(2,1)}, bf16[128,2,8,128]{3,2,1,0:T(8,128)(2,1)}) custom-call(s32[2]{0:T(128)} %pad_add_fusion.even, bf16[24,16,16,128]{3,2,1,0:T(8,128)(2,1)} %bitcast.14, bf16[24,16,16,128]{3,2,1,0:T(8,128)(2,1)} %bitcast.15, ...), custom_call_target="tpu_custom_call" | custom-call | tf_op jit(solution)/shard_map/columns/pallas_call | solution.py:150
  40.7 0.0 collective-permute-done.3.x.a
  40.7 0.0 collective-permute-done.4.y.b
  40.7 0.8 copy-done
  41.5 0.2 copy-done.1
  41.7 2.8 %corners.1 = (bf16[128,2,8,128]{3,2,1,0:T(8,128)(2,1)}, bf16[128,2,8,128]{3,2,1,0:T(8,128)(2,1)}, bf16[128,2,8,128]{3,2,1,0:T(8,128)(2,1)}, bf16[128,2,8,128]{3,2,1,0:T(8,128)(2,1)}) custom-call(s32[2]{0:T(128)} %pad_add_fusion.even, bf16[64,2,16,128]{3,2,1,0:T(8,128)(2,1)} %copy-done, ...), custom_call_target="tpu_custom_call", output_to_operand_aliasing={{0}: (3, {}), {1}: (4, {}), {2}: (5, {}), {3}: (6, {})} | custom-call | tf_op jit(solution)/shard_map/corners/pallas_call | solution.py:186
  44.5 1.6 %collective-permute-start.13 = (bf16[128,2,8,128]{3,2,1,0:T(8,128)(2,1)}, bf16[128,2,8,128]{3,2,1,0:T(8,128)(2,1)S(1)}, u32[]{:S(2)}, u32[]{:S(2)}) collective-permute-start(bf16[128,2,8,128]{3,2,1,0:T(8,128)(2,1)} %get-tuple-element.85), channel_id=1, source_target_pairs={{0,2},{2,0},{4,6},{6,4},{8,10},{10,8},{12,14},{14,12},{16,18},{18,... | collective-permute-start | bytes 1572872 | tf_op jit(solution)/shard_map/ppermute | solution.py:60
  46.1 4.3 %collective-permute-start.14 = (bf16[128,2,8,128]{3,2,1,0:T(8,128)(2,1)}, bf16[128,2,8,128]{3,2,1,0:T(8,128)(2,1)S(1)}, u32[]{:S(2)}, u32[]{:S(2)}) collective-permute-start(bf16[128,2,8,128]{3,2,1,0:T(8,128)(2,1)} %get-tuple-element.86), channel_id=1, source_target_pairs={{0,0},{2,4},{4,2},{6,8},{8,6},{10,12},{12,10},{14,14},{16,16},{18,... | collective-permute-start | bytes 1572872 | tf_op jit(solution)/shard_map/ppermute | solution.py:60
  50.4 0.5 collective-permute-start.11
  50.9 3.4 %collective-permute-start.12 = (bf16[128,2,8,128]{3,2,1,0:T(8,128)(2,1)}, bf16[128,2,8,128]{3,2,1,0:T(8,128)(2,1)}, u32[]{:S(2)}, u32[]{:S(2)}) collective-permute-start(bf16[128,2,8,128]{3,2,1,0:T(8,128)(2,1)} %get-tuple-element.83), channel_id=1, source_target_pairs={{0,0},{2,4},{4,2},{6,8},{8,6},{10,12},{12,10},{14,14},{16,16},{18,... | collective-permute-start | bytes 1572872 | tf_op jit(solution)/shard_map/ppermute | solution.py:60
  54.3 1.1 fusion.16.bias
  55.4 2.7 %halo_to_heads.1 = (bf16[16,2,64,128]{3,2,1,0:T(8,128)(2,1)}, bf16[16,2,64,128]{3,2,1,0:T(8,128)(2,1)}) custom-call(s32[2]{0:T(128)} %pad_add_fusion.even, bf16[64,2,16,128]{3,2,1,0:T(8,128)(2,1)} %copy-done, bf16[64,2,16,128]{3,2,1,0:T(8,128)(2,1)} %copy-done.1), custom_call_target="tpu_custom_call" | custom-call | tf_op jit(solution)/shard_map/halo_to_heads/pallas_call | solution.py:107
  58.1 3.5 %far_heads.1.far = bf16[16,2,256,128]{3,2,1,0:T(8,128)(2,1)} custom-call(bf16[64,2,16,128]{3,2,1,0:T(8,128)(2,1)} %copy-done.2, bf16[64,2,16,128]{3,2,1,0:T(8,128)(2,1)} %collective-permute-done.8.refs_1_, bf16[64,2,16,128]{3,2,1,0:T(8,128)(2,1)} %collective-permute-done.9.refs_2_, bf16[64,2,16,128]{3,2,1,0:T(8,128)(2,1)} %collective-permute-done.10.refs_3_), custom_call_target="tpu_custom_call" | custom-call | tf_op jit(solution)/shard_map/far_heads/pallas_call | solution.py:126
  61.6 1.1 collective-permute-done.13.sa
  62.7 2.4 %collective-permute-done.14.sb = bf16[128,2,8,128]{3,2,1,0:T(8,128)(2,1)S(1)} collective-permute-done((bf16[128,2,8,128]{3,2,1,0:T(8,128)(2,1)}, bf16[128,2,8,128]{3,2,1,0:T(8,128)(2,1)S(1)}, u32[]{:S(2)}, u32[]{:S(2)}) %collective-permute-start.14) | collective-permute-done | bytes 524320 | tf_op jit(solution)/shard_map/ppermute | solution.py:60
  65.1 0.8 copy-done.7
  65.9 11.9 %attend.3 = (bf16[8,384,128]{2,1,0:T(8,128)(2,1)}, bf16[8,384,128]{2,1,0:T(8,128)(2,1)}, bf16[8,2,384,128]{3,2,1,0:T(8,128)(2,1)}, bf16[8,2,64,128]{3,2,1,0:T(8,...) custom-call(bf16[16,384,128]{2,1,0:T(8,128)(2,1)} %get-tuple-element., ...), custom_call_target="tpu_custom_call" | custom-call | flops 2617245696 | bytes 12582912 | tf_op jit(solution)/shard_map/attend/pallas_call | solution.py:409
  77.8 0.1 collective-permute-start.16
  77.9 4.4 %collective-permute-start.18 = (bf16[8,2,128,128]{3,2,1,0:T(8,128)(2,1)}, bf16[8,2,128,128]{3,2,1,0:T(8,128)(2,1)S(1)}, u32[]{:S(2)}, u32[]{:S(2)}) collective-permute-start(bf16[8,2,128,128]{3,2,1,0:T(8,128)(2,1)} %get-tuple-element.97), channel_id=1, source_target_pairs={{0,0},{2,4},{4,2},{6,8},{8,6},{10,12},{12,10},{14,14},{16,16},{18,... | collective-permute-start | bytes 1572872 | tf_op jit(solution)/shard_map/ppermute | solution.py:60
  82.3 11.8 %attend.2 = (bf16[8,384,128]{2,1,0:T(8,128)(2,1)}, bf16[8,384,128]{2,1,0:T(8,128)(2,1)}, bf16[8,2,384,128]{3,2,1,0:T(8,128)(2,1)}, bf16[8,2,64,128]{3,2,1,0:T(8,...) custom-call(bf16[16,384,128]{2,1,0:T(8,128)(2,1)} %get-tuple-element., ...), custom_call_target="tpu_custom_call" | custom-call | flops 2617245696 | bytes 12582912 | tf_op jit(solution)/shard_map/attend/pallas_call | solution.py:409
  94.1 0.1 collective-permute-start.15
  94.2 3.9 %collective-permute-start.17 = (bf16[8,2,128,128]{3,2,1,0:T(8,128)(2,1)}, bf16[8,2,128,128]{3,2,1,0:T(8,128)(2,1)}, u32[]{:S(2)}, u32[]{:S(2)}) collective-permute-start(bf16[8,2,128,128]{3,2,1,0:T(8,128)(2,1)} %get-tuple-element.96), channel_id=1, source_target_pairs={{0,0},{2,4},{4,2},{6,8},{8,6},{10,12},{12,10},{14,14},{16,16},{18,... | collective-permute-start | bytes 1572872 | tf_op jit(solution)/shard_map/ppermute | solution.py:60
  98.1 0.8 copy-done.3
  98.9 0.2 copy-done.4
  99.1 2.6 %fold.3 = (bf16[64,2,8,128]{3,2,1,0:T(8,128)(2,1)}, bf16[64,2,8,128]{3,2,1,0:T(8,128)(2,1)}) custom-call(s32[2]{0:T(128)} %pad_add_fusion.even, bf16[8,2,64,128]{3,2,1,0:T(8,128)(2,1)} %get-tuple-element.103.gup, bf16[8,2,64,128]{3,2,1,0:T(8,128)(2,1)} %get-tuple-element.104.gdn, bf16[8,2,128,128]{3,2,1,0:T(8,128)(2,1)} %copy-done.3, ...), custom_call_target="tpu_custom_call" | custom-call | tf_op jit(solution)/shard_map/fold/pallas_call | solution.py:241
  101.7 2.8 %collective-permute-start.20 = (bf16[64,2,8,128]{3,2,1,0:T(8,128)(2,1)}, bf16[64,2,8,128]{3,2,1,0:T(8,128)(2,1)S(1)}, u32[]{:S(2)}, u32[]{:S(2)}) collective-permute-start(bf16[64,2,8,128]{3,2,1,0:T(8,128)(2,1)} %get-tuple-element.105), channel_id=1, source_target_pairs={{0,16},{2,18},{4,20},{6,22},{8,24},{10,26},{12,28},{14,30},{16,0},... | collective-permute-start | bytes 786440 | tf_op jit(solution)/shard_map/ppermute | solution.py:60
  104.5 4.0 %collective-permute-start.22 = (bf16[64,2,8,128]{3,2,1,0:T(8,128)(2,1)}, bf16[64,2,8,128]{3,2,1,0:T(8,128)(2,1)S(1)}, u32[]{:S(2)}, u32[]{:S(2)}) collective-permute-start(bf16[64,2,8,128]{3,2,1,0:T(8,128)(2,1)} %get-tuple-element.107), channel_id=1, source_target_pairs={{0,0},{2,2},{4,4},{6,6},{8,8},{10,10},{12,12},{14,14},{16,32},{18,... | collective-permute-start | bytes 786440 | tf_op jit(solution)/shard_map/ppermute | solution.py:60
  108.5 4.8 %collective-permute-done.17.refs_4_.from_b = bf16[8,2,128,128]{3,2,1,0:T(8,128)(2,1)} collective-permute-done((bf16[8,2,128,128]{3,2,1,0:T(8,128)(2,1)}, bf16[8,2,128,128]{3,2,1,0:T(8,128)(2,1)}, u32[]{:S(2)}, u32[]{:S(2)}) %collective-permute-start.17) | collective-permute-done | bytes 524320 | tf_op jit(solution)/shard_map/ppermute | solution.py:60
  113.4 2.6 %fold.2 = (bf16[64,2,8,128]{3,2,1,0:T(8,128)(2,1)}, bf16[64,2,8,128]{3,2,1,0:T(8,128)(2,1)}) custom-call(s32[2]{0:T(128)} %pad_add_fusion.even, bf16[8,2,64,128]{3,2,1,0:T(8,128)(2,1)} %get-tuple-element.100.gup, bf16[8,2,64,128]{3,2,1,0:T(8,128)(2,1)} %get-tuple-element.101.gdn, bf16[8,2,128,128]{3,2,1,0:T(8,128)(2,1)} %copy-done.5, ...), custom_call_target="tpu_custom_call" | custom-call | tf_op jit(solution)/shard_map/fold/pallas_call | solution.py:241
  116.0 10.8 %collective-permute-start.19 = (bf16[64,2,8,128]{3,2,1,0:T(8,128)(2,1)}, bf16[64,2,8,128]{3,2,1,0:T(8,128)(2,1)S(1)}, u32[]{:S(2)}, u32[]{:S(2)}) collective-permute-start(bf16[64,2,8,128]{3,2,1,0:T(8,128)(2,1)} %get-tuple-element.102), channel_id=1, source_target_pairs={{0,16},{2,18},{4,20},{6,22},{8,24},{10,26},{12,28},{14,30},{16,0},... | collective-permute-start | bytes 786440 | tf_op jit(solution)/shard_map/ppermute | solution.py:60
  126.8 3.5 %collective-permute-start.21 = (bf16[64,2,8,128]{3,2,1,0:T(8,128)(2,1)}, bf16[64,2,8,128]{3,2,1,0:T(8,128)(2,1)S(1)}, u32[]{:S(2)}, u32[]{:S(2)}) collective-permute-start(bf16[64,2,8,128]{3,2,1,0:T(8,128)(2,1)} %get-tuple-element.106), channel_id=1, source_target_pairs={{0,0},{2,2},{4,4},{6,6},{8,8},{10,10},{12,12},{14,14},{16,32},{18,... | collective-permute-start | bytes 786440 | tf_op jit(solution)/shard_map/ppermute | solution.py:60
  130.3 4.0 %to_tokens.1 = (bf16[1,384,16,128]{3,2,1,0:T(8,128)(2,1)}, bf16[1,384,16,128]{3,2,1,0:T(8,128)(2,1)}) custom-call(bf16[8,384,128]{2,1,0:T(8,128)(2,1)} %get-tuple-element.84.refs_0_, bf16[8,384,128]{2,1,0:T(8,128)(2,1)} %get-tuple-element.87.refs_1_, bf16[8,384,128]{2,1,0:T(8,128)(2,1)} %get-tuple-element.88.refs_2_, ...), custom_call_target="tpu_custom_call" | custom-call | tf_op jit(solution)/shard_map/to_tokens/pallas_call | solution.py:211
  134.2 5.7 %premerge.1 = (bf16[1,384,16,128]{3,2,1,0:T(8,128)(2,1)}, bf16[1,384,16,128]{3,2,1,0:T(8,128)(2,1)}) custom-call(s32[2]{0:T(128)} %pad_add_fusion.even, bf16[8,2,384,128]{3,2,1,0:T(8,128)(2,1)} %get-tuple-element.92.refs_0_, bf16[8,2,384,128]{3,2,1,0:T(8,128)(2,1)} %get-tuple-element.93.refs_1_, bf16[8,2,128,128]{3,2,1,0:T(8,128)(2,1)} %copy-done.5, ...), custom_call_target="tpu_custom_call" | custom-call | tf_op jit(solution)/shard_map/premerge/pallas_call | solution.py:272
  140.0 0.6 copy-done.8
  140.6 0.1 copy-done.9
  140.7 0.1 copy-done.10
  140.8 0.1 copy-done.11
  140.9 3.2 %finish.1 = (bf16[1,384,16,128]{3,2,1,0:T(8,128)(2,1)}, bf16[1,384,16,128]{3,2,1,0:T(8,128)(2,1)}) custom-call(s32[2]{0:T(128)} %pad_add_fusion.even, bf16[1,384,16,128]{3,2,1,0:T(8,128)(2,1)} %get-tuple-element.98.refs_0_, bf16[1,384,16,128]{3,2,1,0:T(8,128)(2,1)} %get-tuple-element.99.refs_1_, ...), custom_call_target="tpu_custom_call", output_to_operand_aliasing={{0}: (1, {}), {1}: (2, {})} | custom-call | tf_op jit(solution)/shard_map/finish/pallas_call | solution.py:299
  (42 shorter events, 0.2 us)
Async XLA Ops:
  1.4 7.2 %collective-permute-start.2 = (bf16[4,2,16,128]{3,2,1,0:T(8,128)(2,1)S(1)}, bf16[4,2,16,128]{3,2,1,0:T(8,128)(2,1)S(1)}, u32[]{:S(2)}, u32[]{:S(2)}) collective-permute-start(bf16[4,2,16,128]{3,2,1,0:T(8,128)(2,1)S(1)} %pad_maximum_fusion.4), channel_id=1, source_target_pairs={{0,24},{2,26},{4,28},{6,30},{8,16},{10,18},{12,20},{14,22},{16,8},... | collective-permute-start | bytes 98312 | tf_op jit(solution)/shard_map/ppermute | solution.py:68
  3.6 5.4 %collective-permute-start.1 = (bf16[4,2,16,128]{3,2,1,0:T(8,128)(2,1)S(1)}, bf16[4,2,16,128]{3,2,1,0:T(8,128)(2,1)S(1)}, u32[]{:S(2)}, u32[]{:S(2)}) collective-permute-start(bf16[4,2,16,128]{3,2,1,0:T(8,128)(2,1)S(1)} %pad_maximum_fusion.4), channel_id=1, source_target_pairs={{0,16},{2,18},{4,20},{6,22},{8,24},{10,26},{12,28},{14,30},{16,0},... | collective-permute-start | bytes 98312 | tf_op jit(solution)/shard_map/ppermute | solution.py:68
  4.3 4.7 %collective-permute-start = (bf16[4,2,16,128]{3,2,1,0:T(8,128)(2,1)S(1)}, bf16[4,2,16,128]{3,2,1,0:T(8,128)(2,1)S(1)}, u32[]{:S(2)}, u32[]{:S(2)}) collective-permute-start(bf16[4,2,16,128]{3,2,1,0:T(8,128)(2,1)S(1)} %pad_maximum_fusion.4), channel_id=1, source_target_pairs={{0,8},{2,10},{4,12},{6,14},{8,0},{10,2},{12,4},{14,6},{16,24},{18,... | collective-permute-start | bytes 98312 | tf_op jit(solution)/shard_map/ppermute | solution.py:68
  6.9 2.1 %copy-start.12 = (bf16[1,4,16,128]{3,2,1,0:T(8,128)(2,1)S(1)}, bf16[1,4,16,128]{3,2,1,0:T(8,128)(2,1)}, u32[]{:S(2)}) copy-start(bf16[1,4,16,128]{3,2,1,0:T(8,128)(2,1)} %param.10) | copy-start | bytes 49156
  6.9 2.1 %copy-start.13 = (bf16[1,4,16,128]{3,2,1,0:T(8,128)(2,1)S(1)}, bf16[1,4,16,128]{3,2,1,0:T(8,128)(2,1)}, u32[]{:S(2)}) copy-start(bf16[1,4,16,128]{3,2,1,0:T(8,128)(2,1)} %param.9) | copy-start | bytes 49156
  9.0 11.3 %collective-permute-start.7 = (bf16[16,2,16,128]{3,2,1,0:T(8,128)(2,1)S(1)}, bf16[16,2,16,128]{3,2,1,0:T(8,128)(2,1)S(1)}, u32[]{:S(2)}, u32[]{:S(2)}) collective-permute-start(bf16[16,2,16,128]{3,2,1,0:T(8,128)(2,1)S(1)} %pad_maximum_fusion.3), channel_id=1, source_target_pairs={{0,96},{2,98},{4,100},{6,102},{8,104},{10,106},{12,108},{14,110},{... | collective-permute-start | bytes 393224 | tf_op jit(solution)/shard_map/ppermute | solution.py:68
  13.4 9.7 %collective-permute-start.6 = (bf16[16,2,16,128]{3,2,1,0:T(8,128)(2,1)S(1)}, bf16[16,2,16,128]{3,2,1,0:T(8,128)(2,1)S(1)}, u32[]{:S(2)}, u32[]{:S(2)}) collective-permute-start(bf16[16,2,16,128]{3,2,1,0:T(8,128)(2,1)S(1)} %pad_maximum_fusion.3), channel_id=1, source_target_pairs={{0,64},{2,66},{4,68},{6,70},{8,72},{10,74},{12,76},{14,78},{16,80}... | collective-permute-start | bytes 393224 | tf_op jit(solution)/shard_map/ppermute | solution.py:68
  13.4 9.7 %collective-permute-start.5 = (bf16[16,2,16,128]{3,2,1,0:T(8,128)(2,1)S(1)}, bf16[16,2,16,128]{3,2,1,0:T(8,128)(2,1)S(1)}, u32[]{:S(2)}, u32[]{:S(2)}) collective-permute-start(bf16[16,2,16,128]{3,2,1,0:T(8,128)(2,1)S(1)} %pad_maximum_fusion.3), channel_id=1, source_target_pairs={{0,32},{2,34},{4,36},{6,38},{8,40},{10,42},{12,44},{14,46},{16,48}... | collective-permute-start | bytes 393224 | tf_op jit(solution)/shard_map/ppermute | solution.py:68
  14.1 26.6 %collective-permute-start.3 = (bf16[64,2,16,128]{3,2,1,0:T(8,128)(2,1)}, bf16[64,2,16,128]{3,2,1,0:T(8,128)(2,1)S(1)}, u32[]{:S(2)}, u32[]{:S(2)}) collective-permute-start(bf16[64,2,16,128]{3,2,1,0:T(8,128)(2,1)} %pad_maximum_fusion), channel_id=1, source_target_pairs={{0,16},{2,18},{4,20},{6,22},{8,24},{10,26},{12,28},{14,30},{16,0},... | collective-permute-start | bytes 1572872 | tf_op jit(solution)/shard_map/ppermute | solution.py:60
  15.5 25.2 %collective-permute-start.4 = (bf16[64,2,16,128]{3,2,1,0:T(8,128)(2,1)}, bf16[64,2,16,128]{3,2,1,0:T(8,128)(2,1)S(1)}, u32[]{:S(2)}, u32[]{:S(2)}) collective-permute-start(bf16[64,2,16,128]{3,2,1,0:T(8,128)(2,1)} %pad_maximum_fusion.1), channel_id=1, source_target_pairs={{0,0},{2,2},{4,4},{6,6},{8,8},{10,10},{12,12},{14,14},{16,32},{18,... | collective-permute-start | bytes 1572872 | tf_op jit(solution)/shard_map/ppermute | solution.py:60
  23.2 9.6 %copy-start.2 = (bf16[64,2,16,128]{3,2,1,0:T(8,128)(2,1)}, bf16[64,2,16,128]{3,2,1,0:T(8,128)(2,1)S(1)}, u32[]{:S(2)}) copy-start(bf16[64,2,16,128]{3,2,1,0:T(8,128)(2,1)S(1)} %pad_maximum_fusion.2.refs_0_) | copy-start | bytes 1572868
  23.2 27.2 %collective-permute-start.10 = (bf16[64,2,16,128]{3,2,1,0:T(8,128)(2,1)S(1)}, bf16[64,2,16,128]{3,2,1,0:T(8,128)(2,1)}, u32[]{:S(2)}, u32[]{:S(2)}) collective-permute-start(bf16[64,2,16,128]{3,2,1,0:T(8,128)(2,1)S(1)} %pad_maximum_fusion.2.refs_0_), channel_id=1, source_target_pairs={{0,6},{2,4},{4,2},{6,0},{8,14},{10,12},{12,10},{14,8},{16,22},{18,... | collective-permute-start | bytes 1572872 | tf_op jit(solution)/shard_map/ppermute | solution.py:68
  26.3 24.6 %collective-permute-start.9 = (bf16[64,2,16,128]{3,2,1,0:T(8,128)(2,1)S(1)}, bf16[64,2,16,128]{3,2,1,0:T(8,128)(2,1)}, u32[]{:S(2)}, u32[]{:S(2)}) collective-permute-start(bf16[64,2,16,128]{3,2,1,0:T(8,128)(2,1)S(1)} %pad_maximum_fusion.2.refs_0_), channel_id=1, source_target_pairs={{0,4},{2,6},{4,0},{6,2},{8,12},{10,14},{12,8},{14,10},{16,20},{18,... | collective-permute-start | bytes 1572872 | tf_op jit(solution)/shard_map/ppermute | solution.py:68
  27.6 30.5 %collective-permute-start.8 = (bf16[64,2,16,128]{3,2,1,0:T(8,128)(2,1)S(1)}, bf16[64,2,16,128]{3,2,1,0:T(8,128)(2,1)}, u32[]{:S(2)}, u32[]{:S(2)}) collective-permute-start(bf16[64,2,16,128]{3,2,1,0:T(8,128)(2,1)S(1)} %pad_maximum_fusion.2.refs_0_), channel_id=1, source_target_pairs={{0,2},{2,0},{4,6},{6,4},{8,10},{10,8},{12,14},{14,12},{16,18},{18,... | collective-permute-start | bytes 1572872 | tf_op jit(solution)/shard_map/ppermute | solution.py:68
  40.7 0.8 copy-start
  40.7 0.9 copy-start.1
  44.5 18.2 %collective-permute-start.13 = (bf16[128,2,8,128]{3,2,1,0:T(8,128)(2,1)}, bf16[128,2,8,128]{3,2,1,0:T(8,128)(2,1)S(1)}, u32[]{:S(2)}, u32[]{:S(2)}) collective-permute-start(bf16[128,2,8,128]{3,2,1,0:T(8,128)(2,1)} %get-tuple-element.85), channel_id=1, source_target_pairs={{0,2},{2,0},{4,6},{6,4},{8,10},{10,8},{12,14},{14,12},{16,18},{18,... | collective-permute-start | bytes 1572872 | tf_op jit(solution)/shard_map/ppermute | solution.py:60
  46.1 19.1 %collective-permute-start.14 = (bf16[128,2,8,128]{3,2,1,0:T(8,128)(2,1)}, bf16[128,2,8,128]{3,2,1,0:T(8,128)(2,1)S(1)}, u32[]{:S(2)}, u32[]{:S(2)}) collective-permute-start(bf16[128,2,8,128]{3,2,1,0:T(8,128)(2,1)} %get-tuple-element.86), channel_id=1, source_target_pairs={{0,0},{2,4},{4,2},{6,8},{8,6},{10,12},{12,10},{14,14},{16,16},{18,... | collective-permute-start | bytes 1572872 | tf_op jit(solution)/shard_map/ppermute | solution.py:60
  50.4 31.8 %collective-permute-start.11 = (bf16[128,2,8,128]{3,2,1,0:T(8,128)(2,1)}, bf16[128,2,8,128]{3,2,1,0:T(8,128)(2,1)}, u32[]{:S(2)}, u32[]{:S(2)}) collective-permute-start(bf16[128,2,8,128]{3,2,1,0:T(8,128)(2,1)} %get-tuple-element.82), channel_id=1, source_target_pairs={{0,2},{2,0},{4,6},{6,4},{8,10},{10,8},{12,14},{14,12},{16,18},{18,... | collective-permute-start | bytes 1572872 | tf_op jit(solution)/shard_map/ppermute | solution.py:60
  50.9 31.3 %collective-permute-start.12 = (bf16[128,2,8,128]{3,2,1,0:T(8,128)(2,1)}, bf16[128,2,8,128]{3,2,1,0:T(8,128)(2,1)}, u32[]{:S(2)}, u32[]{:S(2)}) collective-permute-start(bf16[128,2,8,128]{3,2,1,0:T(8,128)(2,1)} %get-tuple-element.83), channel_id=1, source_target_pairs={{0,0},{2,4},{4,2},{6,8},{8,6},{10,12},{12,10},{14,14},{16,16},{18,... | collective-permute-start | bytes 1572872 | tf_op jit(solution)/shard_map/ppermute | solution.py:60
  62.7 2.4 %copy-start.6 = (bf16[128,2,8,128]{3,2,1,0:T(8,128)(2,1)}, bf16[128,2,8,128]{3,2,1,0:T(8,128)(2,1)S(1)}, u32[]{:S(2)}) copy-start(bf16[128,2,8,128]{3,2,1,0:T(8,128)(2,1)S(1)} %collective-permute-done.13.sa) | copy-start | bytes 1572868
  65.1 0.8 copy-start.7
  77.8 20.3 %collective-permute-start.16 = (bf16[8,2,128,128]{3,2,1,0:T(8,128)(2,1)}, bf16[8,2,128,128]{3,2,1,0:T(8,128)(2,1)S(1)}, u32[]{:S(2)}, u32[]{:S(2)}) collective-permute-start(bf16[8,2,128,128]{3,2,1,0:T(8,128)(2,1)} %get-tuple-element.95), channel_id=1, source_target_pairs={{0,2},{2,0},{4,6},{6,4},{8,10},{10,8},{12,14},{14,12},{16,18},{18,... | collective-permute-start | bytes 1572872 | tf_op jit(solution)/shard_map/ppermute | solution.py:60
  77.9 20.2 %collective-permute-start.18 = (bf16[8,2,128,128]{3,2,1,0:T(8,128)(2,1)}, bf16[8,2,128,128]{3,2,1,0:T(8,128)(2,1)S(1)}, u32[]{:S(2)}, u32[]{:S(2)}) collective-permute-start(bf16[8,2,128,128]{3,2,1,0:T(8,128)(2,1)} %get-tuple-element.97), channel_id=1, source_target_pairs={{0,0},{2,4},{4,2},{6,8},{8,6},{10,12},{12,10},{14,14},{16,16},{18,... | collective-permute-start | bytes 1572872 | tf_op jit(solution)/shard_map/ppermute | solution.py:60
  94.1 14.4 %collective-permute-start.15 = (bf16[8,2,128,128]{3,2,1,0:T(8,128)(2,1)}, bf16[8,2,128,128]{3,2,1,0:T(8,128)(2,1)S(1)}, u32[]{:S(2)}, u32[]{:S(2)}) collective-permute-start(bf16[8,2,128,128]{3,2,1,0:T(8,128)(2,1)} %get-tuple-element.94), channel_id=1, source_target_pairs={{0,2},{2,0},{4,6},{6,4},{8,10},{10,8},{12,14},{14,12},{16,18},{18,... | collective-permute-start | bytes 1572872 | tf_op jit(solution)/shard_map/ppermute | solution.py:60
  94.2 19.2 %collective-permute-start.17 = (bf16[8,2,128,128]{3,2,1,0:T(8,128)(2,1)}, bf16[8,2,128,128]{3,2,1,0:T(8,128)(2,1)}, u32[]{:S(2)}, u32[]{:S(2)}) collective-permute-start(bf16[8,2,128,128]{3,2,1,0:T(8,128)(2,1)} %get-tuple-element.96), channel_id=1, source_target_pairs={{0,0},{2,4},{4,2},{6,8},{8,6},{10,12},{12,10},{14,14},{16,16},{18,... | collective-permute-start | bytes 1572872 | tf_op jit(solution)/shard_map/ppermute | solution.py:60
  98.1 0.8 copy-start.3
  98.1 1.0 copy-start.4
  101.7 38.2 %collective-permute-start.20 = (bf16[64,2,8,128]{3,2,1,0:T(8,128)(2,1)}, bf16[64,2,8,128]{3,2,1,0:T(8,128)(2,1)S(1)}, u32[]{:S(2)}, u32[]{:S(2)}) collective-permute-start(bf16[64,2,8,128]{3,2,1,0:T(8,128)(2,1)} %get-tuple-element.105), channel_id=1, source_target_pairs={{0,16},{2,18},{4,20},{6,22},{8,24},{10,26},{12,28},{14,30},{16,0},... | collective-permute-start | bytes 786440 | tf_op jit(solution)/shard_map/ppermute | solution.py:60
  104.5 35.4 %collective-permute-start.22 = (bf16[64,2,8,128]{3,2,1,0:T(8,128)(2,1)}, bf16[64,2,8,128]{3,2,1,0:T(8,128)(2,1)S(1)}, u32[]{:S(2)}, u32[]{:S(2)}) collective-permute-start(bf16[64,2,8,128]{3,2,1,0:T(8,128)(2,1)} %get-tuple-element.107), channel_id=1, source_target_pairs={{0,0},{2,2},{4,4},{6,6},{8,8},{10,10},{12,12},{14,14},{16,32},{18,... | collective-permute-start | bytes 786440 | tf_op jit(solution)/shard_map/ppermute | solution.py:60
  108.5 4.8 %copy-start.5 = (bf16[8,2,128,128]{3,2,1,0:T(8,128)(2,1)}, bf16[8,2,128,128]{3,2,1,0:T(8,128)(2,1)S(1)}, u32[]{:S(2)}) copy-start(bf16[8,2,128,128]{3,2,1,0:T(8,128)(2,1)S(1)} %collective-permute-done.15.refs_2_.from_a) | copy-start | bytes 1572868
  116.0 23.9 %collective-permute-start.19 = (bf16[64,2,8,128]{3,2,1,0:T(8,128)(2,1)}, bf16[64,2,8,128]{3,2,1,0:T(8,128)(2,1)S(1)}, u32[]{:S(2)}, u32[]{:S(2)}) collective-permute-start(bf16[64,2,8,128]{3,2,1,0:T(8,128)(2,1)} %get-tuple-element.102), channel_id=1, source_target_pairs={{0,16},{2,18},{4,20},{6,22},{8,24},{10,26},{12,28},{14,30},{16,0},... | collective-permute-start | bytes 786440 | tf_op jit(solution)/shard_map/ppermute | solution.py:60
  126.8 13.2 %collective-permute-start.21 = (bf16[64,2,8,128]{3,2,1,0:T(8,128)(2,1)}, bf16[64,2,8,128]{3,2,1,0:T(8,128)(2,1)S(1)}, u32[]{:S(2)}, u32[]{:S(2)}) collective-permute-start(bf16[64,2,8,128]{3,2,1,0:T(8,128)(2,1)} %get-tuple-element.106), channel_id=1, source_target_pairs={{0,0},{2,2},{4,4},{6,6},{8,8},{10,10},{12,12},{14,14},{16,32},{18,... | collective-permute-start | bytes 786440 | tf_op jit(solution)/shard_map/ppermute | solution.py:60
  139.9 0.7 copy-start.8
  139.9 0.8 copy-start.9
  139.9 0.9 copy-start.10
  139.9 0.9 copy-start.11
where the time goes:
time: 146 us; the launch traced here: 144 us
  Pallas kernels  63.2 us (43%)
  starting transfers between devices  58.9 us (40%)
  waiting for transfers between devices  11.6 us (8%)
  local copies, waits for them, and re-layouts  5.08 us (3%)
  other arithmetic  4.31 us (3%)
    ppermute x14, starting transfers between devices, exchange(): return lax.ppermute(value, 'seq', pairs)  45.5 us
    pallas_call x2, Pallas kernels, attend(): pl.pallas_call(functools.partial(attend_kernel, heads), grid=(steps,), in...  23.7 us
    ppermute x9, starting transfers between devices, swapped(): return lax.ppermute(block, 'seq', pairs)  13.4 us
    ppermute x14, waiting for transfers between devices, exchange(): return lax.ppermute(value, 'seq', pairs)  8.39 us
    pallas_call x1, Pallas kernels, premerge(): pl.pallas_call(premerge_kernel, in_specs=[SMEM] + [VMEM] * (3 * CHUNKS),...  5.65 us
    pallas_call x2, Pallas kernels, fold(): pl.pallas_call(fold_kernel, in_specs=[SMEM] + [VMEM] * 4, out_shape=[sds(...  5.18 us
    pallas_call x1, Pallas kernels, pairs_to_heads(): pl.pallas_call(pairs_to_heads_kernel, out_shape=sds(h, 2, t, d), compiler...  4.68 us
    pallas_call x1, Pallas kernels, to_heads(): pl.pallas_call(to_heads_kernel, out_shape=[sds(h, t, d)] * 2, compiler_pa...  4.23 us
  transfers between devices with their start and end apart: 23, of which 5 were waited for; matrix products, arithmetic and copies ran while one was open for 3% of the time, Pallas kernels for 42%

commit v1 on v0

--- a/solution.py
+++ b/solution.py
@@ -77,8 +77,16 @@
 
 def pairs_to_heads(k, v):
     t, h, d = k.shape[1:]
-    return pl.pallas_call(
-        pairs_to_heads_kernel, out_shape=sds(h, 2, t, d), compiler_params=PARAMS, name="pairs_to_heads"
+    n = t // BLOCKS
+    tokens = pl.BlockSpec((1, n, h, d), lambda g: (0, g, 0, 0))
+    return pl.pallas_call(
+        pairs_to_heads_kernel,
+        grid=(BLOCKS,),
+        in_specs=[tokens, tokens],
+        out_specs=pl.BlockSpec((h, 2, n, d), lambda g: (0, 0, g, 0)),
+        out_shape=sds(h, 2, t, d),
+        compiler_params=PARAMS,
+        name="pairs_to_heads",
     )(k, v)
 
 
@@ -89,24 +97,36 @@
 
 def to_heads(x, y):
     t, h, d = x.shape[1:]
-    return pl.pallas_call(
-        to_heads_kernel, out_shape=[sds(h, t, d)] * 2, compiler_params=PARAMS, name="to_heads"
+    n = t // BLOCKS
+    tokens = pl.BlockSpec((1, n, h, d), lambda g: (0, g, 0, 0))
+    heads = pl.BlockSpec((h, n, d), lambda g: (0, g, 0))
+    return pl.pallas_call(
+        to_heads_kernel,
+        grid=(BLOCKS,),
+        in_specs=[tokens, tokens],
+        out_specs=[heads, heads],
+        out_shape=[sds(h, t, d)] * 2,
+        compiler_params=PARAMS,
+        name="to_heads",
     )(x, y)
 
 
 def halo_to_heads_kernel(even, x, y, up, dn):
-    for i in range(2):
-        a = jnp.swapaxes(x[:, i], 0, 1)
-        b = jnp.swapaxes(y[:, i], 0, 1)
-        up[:, i] = lax.select(even[0] == 1, b, a)
-        dn[:, i] = lax.select(even[0] == 1, a, b)
+    a = jnp.swapaxes(x[:, 0], 0, 1)
+    b = jnp.swapaxes(y[:, 0], 0, 1)
+    up[:, 0] = lax.select(even[0] == 1, b, a)
+    dn[:, 0] = lax.select(even[0] == 1, a, b)
 
 
 def halo_to_heads(even, x, y):
     t, _, h, d = x.shape
+    tokens = pl.BlockSpec((t, 1, h, d), lambda g: (0, g, 0, 0))
+    heads = pl.BlockSpec((h, 1, t, d), lambda g: (0, g, 0, 0))
     return pl.pallas_call(
         halo_to_heads_kernel,
-        in_specs=[SMEM, VMEM, VMEM],
+        grid=(2,),
+        in_specs=[SMEM, tokens, tokens],
+        out_specs=[heads, heads],
         out_shape=[sds(h, 2, t, d)] * 2,
         compiler_params=PARAMS,
         name="halo_to_heads",
@@ -117,85 +137,61 @@
     out = refs[-1]
     n = refs[0].shape[0]
     for j, piece in enumerate(refs[:-1]):
-        for i in range(2):
-            out[:, i, j * n : (j + 1) * n] = jnp.swapaxes(piece[:, i], 0, 1)
+        out[:, 0, j * n : (j + 1) * n] = jnp.swapaxes(piece[:, 0], 0, 1)
 
 
 def far_heads(pieces):
     n, _, h, d = pieces[0].shape
-    return pl.pallas_call(
-        far_kernel, out_shape=sds(h, 2, n * len(pieces), d), compiler_params=PARAMS, name="far_heads"
+    t = n * len(pieces)
+    return pl.pallas_call(
+        far_kernel,
+        grid=(2,),
+        in_specs=[pl.BlockSpec((n, 1, h, d), lambda g: (0, g, 0, 0))] * len(pieces),
+        out_specs=pl.BlockSpec((h, 1, t, d), lambda g: (0, g, 0, 0)),
+        out_shape=sds(h, 2, t, d),
+        compiler_params=PARAMS,
+        name="far_heads",
     )(*pieces)
 
 
-def columns_kernel(even, ka, kb, va, vb, *outs):
-    h, d = ka.shape[2:]
+def sides_kernel(even, a, b, ka, kb, va, vb, *outs):
+    h, d = a.shape[2:]
     n = h // CHUNKS
-    for j, mine in enumerate(((ka, va), (kb, vb))):
+    for j, (mine, e) in enumerate((((ka, va), even[1]), ((kb, vb), 1 - even[1]))):
         for i in range(2):
             x = mine[i][...].reshape(SIDE, h, d)
             for c in range(CHUNKS):
                 outs[j * CHUNKS + c][CORNER : CORNER + SIDE, i] = x[:, c * n : (c + 1) * n]
-
-
-def columns(even, k, v):
-    h, d = k.shape[1:]
+            for g, rows in enumerate((a, b)):
+                end = (STRIP - CORNER) * (g ^ even[0])
+                for r in range(RADIUS):
+                    x = rows[pl.ds(r * TILE_W + (TILE_W - RADIUS) * e, RADIUS), i]
+                    for c in range(CHUNKS):
+                        outs[j * CHUNKS + c][pl.ds(end + r * RADIUS, RADIUS), i] = x[:, c * n : (c + 1) * n]
+
+
+def sides(even, a, b, k, v):
+    h, d = a.shape[2:]
     k = k.reshape(TILE_H, TILE_W, h, d)
     v = v.reshape(TILE_H, TILE_W, h, d)
     block = (TILE_H, RADIUS, h, d)
     last = TILE_W // RADIUS - 1
+    whole = pl.BlockSpec(a.shape, lambda g, e: (0, 0, 0, 0))
     side_a = pl.BlockSpec(block, lambda g, e: (0, last * e[1], 0, 0))
     side_b = pl.BlockSpec(block, lambda g, e: (0, last * (1 - e[1]), 0, 0))
     shape = (STRIP, 2, h // CHUNKS, d)
-    return pl.pallas_call(
-        columns_kernel,
+    outs = pl.pallas_call(
+        sides_kernel,
         grid_spec=pltpu.PrefetchScalarGridSpec(
             num_scalar_prefetch=1,
             grid=(1,),
-            in_specs=[side_a, side_b, side_a, side_b],
+            in_specs=[whole, whole, side_a, side_b, side_a, side_b],
             out_specs=[pl.BlockSpec(shape, lambda g, e: (0, 0, 0, 0))] * (2 * CHUNKS),
         ),
         out_shape=[sds(*shape)] * (2 * CHUNKS),
         compiler_params=PARAMS,
-        name="columns",
-    )(even, k, k, v, v)
-
-
-def corners_kernel(even, a, b, *refs):
-    outs = refs[len(refs) // 2 :]
-    h = a.shape[2]
-    n = h // CHUNKS
-    for g, rows in enumerate((a, b)):
-
-        @pl.when(pl.program_id(0) == g)
-        def _():
-            for j, e in enumerate((even[1], 1 - even[1])):
-                for r in range(RADIUS):
-                    start = r * TILE_W + (TILE_W - RADIUS) * e
-                    for i in range(2):
-                        x = rows[pl.ds(start, RADIUS), i]
-                        for c in range(CHUNKS):
-                            out = outs[j * CHUNKS + c]
-                            out[r * RADIUS : (r + 1) * RADIUS, i] = x[:, c * n : (c + 1) * n]
-
-
-def corners(even, a, b, strips):
-    whole = pl.BlockSpec(a.shape, lambda g, e: (0, 0, 0, 0))
-    last = STRIP // CORNER - 1
-    end = pl.BlockSpec((CORNER,) + strips[0].shape[1:], lambda g, e: (last * (g ^ e[0]), 0, 0, 0))
-    outs = pl.pallas_call(
-        corners_kernel,
-        grid_spec=pltpu.PrefetchScalarGridSpec(
-            num_scalar_prefetch=1,
-            grid=(2,),
-            in_specs=[whole, whole] + [pl.BlockSpec(memory_space=pl.ANY)] * len(strips),
-            out_specs=[end] * len(strips),
-        ),
-        out_shape=[sds(*x.shape) for x in strips],
-        input_output_aliases={3 + i: i for i in range(len(strips))},
-        compiler_params=PARAMS,
-        name="corners",
-    )(even, a, b, *strips)
+        name="sides",
+    )(even, a, b, k, k, v, v)
     return outs[:CHUNKS], outs[CHUNKS:]
 
 
@@ -208,43 +204,55 @@
 
 def to_tokens(xs, ys):
     h, t, d = xs[0].shape
+    n = t // BLOCKS
     return pl.pallas_call(
         to_tokens_kernel,
+        grid=(BLOCKS,),
+        in_specs=[pl.BlockSpec((h, n, d), lambda g: (0, g, 0))] * (2 * len(xs)),
+        out_specs=[pl.BlockSpec((1, n, h * len(xs), d), lambda g: (0, g, 0, 0))] * 2,
         out_shape=[sds(1, t, h * len(xs), d)] * 2,
         compiler_params=PARAMS,
         name="to_tokens",
     )(*xs, *ys)
 
 
-def fold_kernel(even, gup, gdn, from_a, from_b, a, b):
-    h, _, t, d = gup.shape
-    for i in range(2):
-        folded = []
-        for g, o in ((gup, 0), (gdn, STRIP - CORNER)):
-            x = jnp.swapaxes(g[:, i], 0, 1).astype(F32).reshape(RADIUS, TILE_W, h, d)
-            sa, sb = (
-                jnp.swapaxes(s[:, i, o : o + CORNER], 0, 1).astype(F32).reshape(RADIUS, RADIUS, h, d)
-                for s in (from_a, from_b)
-            )
-            left = lax.select(even[1] == 1, sb, sa)
-            right = lax.select(even[1] == 1, sa, sb)
-            x = jnp.concatenate(
-                [x[:, :RADIUS] + left, x[:, RADIUS : TILE_W - RADIUS], x[:, TILE_W - RADIUS :] + right], 1
-            )
-            folded.append(x.reshape(t, h, d).astype(BF))
-        a[:, i] = lax.select(even[0] == 1, folded[1], folded[0])
-        b[:, i] = lax.select(even[0] == 1, folded[0], folded[1])
+def fold_kernel(even, *refs):
+    gup, gdn, from_a, from_b = (refs[c * CHUNKS : (c + 1) * CHUNKS] for c in range(4))
+    a, b = refs[4 * CHUNKS :]
+    t, _, h, d = a.shape
+
+    def tokens(parts, rows, cols):
+        x = jnp.concatenate([r[:, 0, rows] for r in parts], 0)
+        return jnp.swapaxes(x, 0, 1).astype(F32).reshape(RADIUS, cols, h, d)
+
+    folded = []
+    for g, o in ((gup, 0), (gdn, STRIP - CORNER)):
+        x = tokens(g, slice(0, t), TILE_W)
+        sa, sb = (tokens(s, slice(o, o + CORNER), RADIUS) for s in (from_a, from_b))
+        left = lax.select(even[1] == 1, sb, sa)
+        right = lax.select(even[1] == 1, sa, sb)
+        x = jnp.concatenate(
+            [x[:, :RADIUS] + left, x[:, RADIUS : TILE_W - RADIUS], x[:, TILE_W - RADIUS :] + right], 1
+        )
+        folded.append(x.reshape(t, h, d).astype(BF))
+    a[:, 0] = lax.select(even[0] == 1, folded[1], folded[0])
+    b[:, 0] = lax.select(even[0] == 1, folded[0], folded[1])
 
 
 def fold(even, gup, gdn, from_a, from_b):
-    h, _, t, d = gup.shape
+    args = (*gup, *gdn, *from_a, *from_b)
+    h, _, t, d = gup[0].shape
+    h *= CHUNKS
     return pl.pallas_call(
         fold_kernel,
-        in_specs=[SMEM] + [VMEM] * 4,
+        grid=(2,),
+        in_specs=[SMEM]
+        + [pl.BlockSpec((x.shape[0], 1) + x.shape[2:], lambda g: (0, g, 0, 0)) for x in args],
+        out_specs=[pl.BlockSpec((t, 1, h, d), lambda g: (0, g, 0, 0))] * 2,
         out_shape=[sds(t, 2, h, d)] * 2,
         compiler_params=PARAMS,
         name="fold",
-    )(even, gup, gdn, from_a, from_b)
+    )(even, *args)
 
 
 def premerge_kernel(even, *refs):
@@ -278,37 +286,33 @@
     )(even, *own, *from_a, *from_b)
 
 
-def finish_kernel(even, *refs):
-    sums = refs[:2]
-    parts = [refs[2 + c * CHUNKS : 2 + (c + 1) * CHUNKS] for c in range(2)]
-    outs = refs[2 + 2 * CHUNKS :]
-    for g in range(2):
+def finish_kernel(even, dk, dv, from_a, from_b, dk_out, dv_out):
+    for g, part in enumerate((from_a, from_b)):
 
         @pl.when(pl.program_id(0) == g)
         def _():
-            for i in range(2):
-                x = jnp.concatenate([r[:, i] for r in parts[g]], 1).astype(F32)
-                outs[i][0] = (sums[i][0].astype(F32) + x).astype(BF)
+            for i, (x, out) in enumerate(((dk, dk_out), (dv, dv_out))):
+                out[0] = (x[0].astype(F32) + part[:, i].astype(F32)).astype(BF)
 
 
 def finish(even, dk, dv, from_a, from_b):
     h, d = dk.shape[2:]
     last = TOKENS // EDGE - 1
     rows = pl.BlockSpec((1, EDGE, h, d), lambda g, e: (0, last * (g ^ e[0]), 0, 0))
-    part = pl.BlockSpec(from_a[0].shape, lambda g, e: (0, 0, 0, 0))
+    part = pl.BlockSpec(from_a.shape, lambda g, e: (0, 0, 0, 0))
     return pl.pallas_call(
         finish_kernel,
         grid_spec=pltpu.PrefetchScalarGridSpec(
             num_scalar_prefetch=1,
             grid=(2,),
-            in_specs=[rows, rows] + [part] * (2 * CHUNKS),
+            in_specs=[rows, rows, part, part],
             out_specs=[rows, rows],
         ),
         out_shape=[sds(*dk.shape)] * 2,
         input_output_aliases={1: 0, 2: 1},
         compiler_params=PARAMS,
         name="finish",
-    )(even, dk, dv, *from_a, *from_b)
+    )(even, dk, dv, from_a, from_b)
 
 
 def attend_kernel(
@@ -454,30 +458,25 @@
         (coarse, fine_queries, out_grad, fine_keys, fine_values)
     )
     pieces = widened(coarse, 1)
-    strips = columns(even, fine_keys[0], fine_values[0])
     queries, cots = to_heads(fine_queries, out_grad)
     kv = pairs_to_heads(fine_keys, fine_values)
-    row_a, row_b, kv, queries, cots, *strips = lax.optimization_barrier(
-        (row_a, row_b, kv, queries, cots, *strips)
-    )
-    sides = corners(even, row_a, row_b, strips)
-    side_a, side_b = ([exchange(x, False, which) for x in xs] for which, xs in enumerate(sides))
+    bias = near_bias()
+    row_a, row_b, kv, queries, cots, bias = lax.optimization_barrier((row_a, row_b, kv, queries, cots, bias))
+    strips = sides(even, row_a, row_b, fine_keys[0], fine_values[0])
+    side_a, side_b = ([exchange(x, False, which) for x in xs] for which, xs in enumerate(strips))
     up, dn = halo_to_heads(even, row_a, row_b)
     far = far_heads(pieces)
-    bias = near_bias()
-    att, dq, own, to_a, to_b, from_a, from_b = ([] for _ in range(7))
+    att, dq, own, gup, gdn, from_a, from_b = ([] for _ in range(7))
     for c in range(CHUNKS):
-        a, b, mine, gup, gdn, ga, gb = attend(
+        a, b, mine, u, n, ga, gb = attend(
             c, even, queries, cots, kv, up, dn, far, side_a[c], side_b[c], bias
         )
         from_a.append(exchange(ga, False, 0))
         from_b.append(exchange(gb, False, 1))
-        att.append(a)
-        dq.append(b)
-        own.append(mine)
-        ra, rb = fold(even, gup, gdn, from_a[c], from_b[c])
-        to_a.append(exchange(ra, True, 0))
-        to_b.append(exchange(rb, True, 1))
+        for xs, x in ((att, a), (dq, b), (own, mine), (gup, u), (gdn, n)):
+            xs.append(x)
+    to_a, to_b = fold(even, gup, gdn, from_a, from_b)
+    to_a, to_b = exchange(to_a, True, 0), exchange(to_b, True, 1)
     attended, query_grad = to_tokens(att, dq)
     dk, dv = premerge(even, own, from_a, from_b)
     key_grad, value_grad = finish(even, dk, dv, to_a, to_b)

time: 146 us -> 138 us (0.945)
  starting transfers between devices: 58.9 us -> 43.4 us
  waiting for transfers between devices: 11.6 us -> 24.1 us
  Pallas kernels: 63.2 us -> 59.5 us
    ppermute x14 -> x12, starting transfers between devices: 45.5 us -> 30.1 us  [exchange(): return lax.ppermute(value, 'seq', pairs)]
    ppermute x14 -> x12, waiting for transfers between devices: 8.39 us -> 21.6 us  [exchange(): return lax.ppermute(value, 'seq', pairs)]
    pallas_call x9 -> x7, Pallas kernels: 30.7 us -> 27 us  [the longest x1 4.85 us: pairs_to_heads(): pl.pallas_call(pairs_to_heads_kernel, grid=(BLOCKS,), in_specs=[tokens, t...]
    unnamed x28 -> x24, local copies, waits for them, and re-layouts: 3.71 us -> 2.74 us
  transfers between devices with their start and end apart: 23 -> 21, of which waited for: 5 -> 8; matrix products, arithmetic and copies ran while one was open for 3% -> 4% of each run, Pallas kernels for 42% -> 39%
where the time goes in v1:
time: 138 us; the launch traced here: 136 us
  Pallas kernels  59.5 us (43%)
  starting transfers between devices  43.4 us (31%)
  waiting for transfers between devices  24.1 us (17%)
  other arithmetic  4.33 us (3%)
  local copies, waits for them, and re-layouts  4.12 us (3%)
    ppermute x12, starting transfers between devices, exchange(): return lax.ppermute(value, 'seq', pairs)  30.1 us
    pallas_call x2, Pallas kernels, attend(): pl.pallas_call(functools.partial(attend_kernel, heads), grid=(steps,), in...  23.7 us
    ppermute x12, waiting for transfers between devices, exchange(): return lax.ppermute(value, 'seq', pairs)  21.6 us
    ppermute x9, starting transfers between devices, swapped(): return lax.ppermute(block, 'seq', pairs)  13.4 us
    pallas_call x1, Pallas kernels, premerge(): pl.pallas_call(premerge_kernel, in_specs=[SMEM] + [VMEM] * (3 * CHUNKS),...  5.65 us
    pallas_call x1, Pallas kernels, pairs_to_heads(): pl.pallas_call(pairs_to_heads_kernel, grid=(BLOCKS,), in_specs=[tokens, t...  4.85 us
    pallas_call x1, Pallas kernels, to_heads(): pl.pallas_call(to_heads_kernel, grid=(BLOCKS,), in_specs=[tokens, tokens]...  4.81 us
    pallas_call x1, Pallas kernels, to_tokens(): pl.pallas_call(to_tokens_kernel, grid=(BLOCKS,), in_specs=[pl.BlockSpec((...  4.64 us
  transfers between devices with their start and end apart: 21, of which 8 were waited for; matrix products, arithmetic and copies ran while one was open for 4% of the time, Pallas kernels for 39%

profile of v1, /device:TPU:6, one launch (start us, length us, event | category | flops | bytes accessed | tf_op | source)
XLA Modules:
  0.0 136.3 jit_solution(13982905785224101203)
XLA Ops:
  0.6 0.7 pad_maximum_fusion.4
  1.4 2.2 %collective-permute-start.2 = (bf16[4,2,16,128]{3,2,1,0:T(8,128)(2,1)S(1)}, bf16[4,2,16,128]{3,2,1,0:T(8,128)(2,1)S(1)}, u32[]{:S(2)}, u32[]{:S(2)}) collective-permute-start(bf16[4,2,16,128]{3,2,1,0:T(8,128)(2,1)S(1)} %pad_maximum_fusion.4), channel_id=1, source_target_pairs={{0,24},{2,26},{4,28},{6,30},{8,16},{10,18},{12,20},{14,22},{16,8},... | collective-permute-start | bytes 98312 | tf_op jit(solution)/shard_map/ppermute | solution.py:68
  3.6 0.7 collective-permute-start.1
  4.3 1.2 collective-permute-start
  5.6 1.4 %dynamic-slice_bitcast_fusion = (bf16[64,1,16,128]{3,2,1,0:T(8,128)(2,1)S(1)}, bf16[64,1,16,128]{3,2,1,0:T(8,128)(2,1)S(1)}, bf16[64,1,16,128]{3,2,1,0:T(8,128)(2,1)S(1)}, bf16[64,1,16,128]{3,2,1,0:T(8,128)(2,1)S(1)}) fusion(bf16[1,384,16,128]{3,2,1,0:T(8,128)(2,1)} %v, s32[]{:T(128)S(6)} %select_n.93, s32[]{:T(128)S(6)} %select_n.92, ...), kind=kLoop, calls=%fused_computation.31 | loop fusion | bytes 2097160 | tf_op jit(solution)/shard_map/stack | solution.py:451
  7.0 0.0 copy-start.10
  7.0 0.0 copy-start.11
  7.0 0.9 pad_maximum_fusion.1
  7.8 0.8 pad_maximum_fusion
  8.7 0.3 collective-permute-done.1
  9.0 0.0 collective-permute-done
  9.0 4.4 %collective-permute-start.7 = (bf16[16,2,16,128]{3,2,1,0:T(8,128)(2,1)S(1)}, bf16[16,2,16,128]{3,2,1,0:T(8,128)(2,1)S(1)}, u32[]{:S(2)}, u32[]{:S(2)}) collective-permute-start(bf16[16,2,16,128]{3,2,1,0:T(8,128)(2,1)S(1)} %pad_maximum_fusion.3), channel_id=1, source_target_pairs={{0,96},{2,98},{4,100},{6,102},{8,104},{10,106},{12,108},{14,110},{... | collective-permute-start | bytes 393224 | tf_op jit(solution)/shard_map/ppermute | solution.py:68
  13.5 0.0 collective-permute-start.6
  13.5 0.7 collective-permute-start.5
  14.1 1.4 %collective-permute-start.3 = (bf16[64,2,16,128]{3,2,1,0:T(8,128)(2,1)}, bf16[64,2,16,128]{3,2,1,0:T(8,128)(2,1)S(1)}, u32[]{:S(2)}, u32[]{:S(2)}) collective-permute-start(bf16[64,2,16,128]{3,2,1,0:T(8,128)(2,1)} %pad_maximum_fusion), channel_id=1, source_target_pairs={{0,16},{2,18},{4,20},{6,22},{8,24},{10,26},{12,28},{14,30},{16,0},... | collective-permute-start | bytes 1572872 | tf_op jit(solution)/shard_map/ppermute | solution.py:60
  15.5 4.8 %collective-permute-start.4 = (bf16[64,2,16,128]{3,2,1,0:T(8,128)(2,1)}, bf16[64,2,16,128]{3,2,1,0:T(8,128)(2,1)S(1)}, u32[]{:S(2)}, u32[]{:S(2)}) collective-permute-start(bf16[64,2,16,128]{3,2,1,0:T(8,128)(2,1)} %pad_maximum_fusion.1), channel_id=1, source_target_pairs={{0,0},{2,2},{4,4},{6,6},{8,8},{10,10},{12,12},{14,14},{16,32},{18,... | collective-permute-start | bytes 1572872 | tf_op jit(solution)/shard_map/ppermute | solution.py:60
  20.4 0.7 pad_add_fusion.even
  21.0 0.0 collective-permute-done.7
  21.0 2.2 %collective-permute-done.6 = bf16[16,2,16,128]{3,2,1,0:T(8,128)(2,1)S(1)} collective-permute-done((bf16[16,2,16,128]{3,2,1,0:T(8,128)(2,1)S(1)}, bf16[16,2,16,128]{3,2,1,0:T(8,128)(2,1)S(1)}, u32[]{:S(2)}, u32[]{:S(2)}) %collective-permute-start.6) | collective-permute-done | bytes 131104 | tf_op jit(solution)/shard_map/ppermute | solution.py:68
  23.2 0.1 pad_maximum_fusion.2.refs_0_
  23.3 3.1 %collective-permute-start.10 = (bf16[64,2,16,128]{3,2,1,0:T(8,128)(2,1)S(1)}, bf16[64,2,16,128]{3,2,1,0:T(8,128)(2,1)}, u32[]{:S(2)}, u32[]{:S(2)}) collective-permute-start(bf16[64,2,16,128]{3,2,1,0:T(8,128)(2,1)S(1)} %pad_maximum_fusion.2.refs_0_), channel_id=1, source_target_pairs={{0,6},{2,4},{4,2},{6,0},{8,14},{10,12},{12,10},{14,8},{16,22},{18,... | collective-permute-start | bytes 1572872 | tf_op jit(solution)/shard_map/ppermute | solution.py:68
  26.4 0.6 collective-permute-start.9
  27.0 1.1 fusion.16.bias
  28.1 0.5 collective-permute-start.8
  28.5 4.8 %pairs_to_heads.1.kv = bf16[16,2,384,128]{3,2,1,0:T(8,128)(2,1)} custom-call(bf16[1,384,16,128]{3,2,1,0:T(8,128)(2,1)} %k, bf16[1,384,16,128]{3,2,1,0:T(8,128)(2,1)} %v), custom_call_target="tpu_custom_call" | custom-call | tf_op jit(solution)/shard_map/pairs_to_heads/pallas_call | solution.py:82
  33.4 4.8 %to_heads.1 = (bf16[16,384,128]{2,1,0:T(8,128)(2,1)}, bf16[16,384,128]{2,1,0:T(8,128)(2,1)}) custom-call(bf16[1,384,16,128]{3,2,1,0:T(8,128)(2,1)} %x, bf16[1,384,16,128]{3,2,1,0:T(8,128)(2,1)} %y), custom_call_target="tpu_custom_call" | custom-call | tf_op jit(solution)/shard_map/to_heads/pallas_call | solution.py:103
  38.2 1.2 collective-permute-done.3.x.a
  39.4 0.8 copy-done.1
  40.1 0.2 copy-done.2
  40.3 4.1 %sides.1 = (bf16[128,2,8,128]{3,2,1,0:T(8,128)(2,1)}, bf16[128,2,8,128]{3,2,1,0:T(8,128)(2,1)}, bf16[128,2,8,128]{3,2,1,0:T(8,128)(2,1)}, bf16[128,2,8,128]{3,2,1,0:T(8,128)(2,1)}) custom-call(s32[2]{0:T(128)} %pad_add_fusion.even, bf16[64,2,16,128]{3,2,1,0:T(8,128)(2,1)} %copy-done.1, bf16[64,2,16,128]{3,2,1,0:T(8,128)(2,1)} %copy-done.2, ...), custom_call_target="tpu_custom_call" | custom-call | tf_op jit(solution)/shard_map/sides/pallas_call | solution.py:183
  44.4 1.6 %collective-permute-start.13 = (bf16[128,2,8,128]{3,2,1,0:T(8,128)(2,1)}, bf16[128,2,8,128]{3,2,1,0:T(8,128)(2,1)S(1)}, u32[]{:S(2)}, u32[]{:S(2)}) collective-permute-start(bf16[128,2,8,128]{3,2,1,0:T(8,128)(2,1)} %get-tuple-element.69), channel_id=1, source_target_pairs={{0,2},{2,0},{4,6},{6,4},{8,10},{10,8},{12,14},{14,12},{16,18},{18,... | collective-permute-start | bytes 1572872 | tf_op jit(solution)/shard_map/ppermute | solution.py:60
  45.9 4.3 %collective-permute-start.14 = (bf16[128,2,8,128]{3,2,1,0:T(8,128)(2,1)}, bf16[128,2,8,128]{3,2,1,0:T(8,128)(2,1)}, u32[]{:S(2)}, u32[]{:S(2)}) collective-permute-start(bf16[128,2,8,128]{3,2,1,0:T(8,128)(2,1)} %get-tuple-element.70), channel_id=1, source_target_pairs={{0,0},{2,4},{4,2},{6,8},{8,6},{10,12},{12,10},{14,14},{16,16},{18,... | collective-permute-start | bytes 1572872 | tf_op jit(solution)/shard_map/ppermute | solution.py:60
  50.3 0.0 collective-permute-done.10.refs_3_
  50.3 0.5 collective-permute-start.11
  50.8 0.0 collective-permute-done.9.refs_2_
  50.8 3.4 %collective-permute-start.12 = (bf16[128,2,8,128]{3,2,1,0:T(8,128)(2,1)}, bf16[128,2,8,128]{3,2,1,0:T(8,128)(2,1)}, u32[]{:S(2)}, u32[]{:S(2)}) collective-permute-start(bf16[128,2,8,128]{3,2,1,0:T(8,128)(2,1)} %get-tuple-element.66), channel_id=1, source_target_pairs={{0,0},{2,4},{4,2},{6,8},{8,6},{10,12},{12,10},{14,14},{16,16},{18,... | collective-permute-start | bytes 1572872 | tf_op jit(solution)/shard_map/ppermute | solution.py:60
  54.2 2.4 %halo_to_heads.1 = (bf16[16,2,64,128]{3,2,1,0:T(8,128)(2,1)}, bf16[16,2,64,128]{3,2,1,0:T(8,128)(2,1)}) custom-call(s32[2]{0:T(128)} %pad_add_fusion.even, bf16[64,2,16,128]{3,2,1,0:T(8,128)(2,1)} %copy-done.1, bf16[64,2,16,128]{3,2,1,0:T(8,128)(2,1)} %copy-done.2), custom_call_target="tpu_custom_call" | custom-call | tf_op jit(solution)/shard_map/halo_to_heads/pallas_call | solution.py:125
  56.6 0.0 collective-permute-done.8.refs_1_
  56.6 3.0 %far_heads.1.far = bf16[16,2,256,128]{3,2,1,0:T(8,128)(2,1)} custom-call(bf16[64,2,16,128]{3,2,1,0:T(8,128)(2,1)} %copy-done, bf16[64,2,16,128]{3,2,1,0:T(8,128)(2,1)} %collective-permute-done.8.refs_1_, bf16[64,2,16,128]{3,2,1,0:T(8,128)(2,1)} %collective-permute-done.9.refs_2_, bf16[64,2,16,128]{3,2,1,0:T(8,128)(2,1)} %collective-permute-done.10.refs_3_), custom_call_target="tpu_custom_call" | custom-call | tf_op jit(solution)/shard_map/far_heads/pallas_call | solution.py:146
  59.6 3.2 %collective-permute-done.13.sa = bf16[128,2,8,128]{3,2,1,0:T(8,128)(2,1)S(1)} collective-permute-done((bf16[128,2,8,128]{3,2,1,0:T(8,128)(2,1)}, bf16[128,2,8,128]{3,2,1,0:T(8,128)(2,1)S(1)}, u32[]{:S(2)}, u32[]{:S(2)}) %collective-permute-start.13) | collective-permute-done | bytes 524320 | tf_op jit(solution)/shard_map/ppermute | solution.py:60
  62.8 2.3 %collective-permute-done.14.sb = bf16[128,2,8,128]{3,2,1,0:T(8,128)(2,1)} collective-permute-done((bf16[128,2,8,128]{3,2,1,0:T(8,128)(2,1)}, bf16[128,2,8,128]{3,2,1,0:T(8,128)(2,1)}, u32[]{:S(2)}, u32[]{:S(2)}) %collective-permute-start.14) | collective-permute-done | bytes 524320 | tf_op jit(solution)/shard_map/ppermute | solution.py:60
  65.1 11.9 %attend.3 = (bf16[8,384,128]{2,1,0:T(8,128)(2,1)}, bf16[8,384,128]{2,1,0:T(8,128)(2,1)}, bf16[8,2,384,128]{3,2,1,0:T(8,128)(2,1)}, bf16[8,2,64,128]{3,2,1,0:T(8,...) custom-call(bf16[16,384,128]{2,1,0:T(8,128)(2,1)} %get-tuple-element., ...), custom_call_target="tpu_custom_call" | custom-call | flops 2617245696 | bytes 12582912 | tf_op jit(solution)/shard_map/attend/pallas_call | solution.py:413
  77.0 0.1 collective-permute-start.16
  77.1 4.3 %collective-permute-start.18 = (bf16[8,2,128,128]{3,2,1,0:T(8,128)(2,1)}, bf16[8,2,128,128]{3,2,1,0:T(8,128)(2,1)S(1)}, u32[]{:S(2)}, u32[]{:S(2)}) collective-permute-start(bf16[8,2,128,128]{3,2,1,0:T(8,128)(2,1)} %get-tuple-element.81), channel_id=1, source_target_pairs={{0,0},{2,4},{4,2},{6,8},{8,6},{10,12},{12,10},{14,14},{16,16},{18,... | collective-permute-start | bytes 1572872 | tf_op jit(solution)/shard_map/ppermute | solution.py:60
  81.5 0.0 copy-start.6
  81.5 0.0 collective-permute-done.12.sb
  81.5 0.8 copy-done.6
  82.3 11.8 %attend.2 = (bf16[8,384,128]{2,1,0:T(8,128)(2,1)}, bf16[8,384,128]{2,1,0:T(8,128)(2,1)}, bf16[8,2,384,128]{3,2,1,0:T(8,128)(2,1)}, bf16[8,2,64,128]{3,2,1,0:T(8,...) custom-call(bf16[16,384,128]{2,1,0:T(8,128)(2,1)} %get-tuple-element., ...), custom_call_target="tpu_custom_call" | custom-call | flops 2617245696 | bytes 12582912 | tf_op jit(solution)/shard_map/attend/pallas_call | solution.py:413
  94.1 0.5 collective-permute-start.15
  94.6 3.5 %collective-permute-start.17 = (bf16[8,2,128,128]{3,2,1,0:T(8,128)(2,1)}, bf16[8,2,128,128]{3,2,1,0:T(8,128)(2,1)}, u32[]{:S(2)}, u32[]{:S(2)}) collective-permute-start(bf16[8,2,128,128]{3,2,1,0:T(8,128)(2,1)} %get-tuple-element.80), channel_id=1, source_target_pairs={{0,0},{2,4},{4,2},{6,8},{8,6},{10,12},{12,10},{14,14},{16,16},{18,... | collective-permute-start | bytes 1572872 | tf_op jit(solution)/shard_map/ppermute | solution.py:60
  98.1 0.0 collective-permute-done.16.refs_3_.refs_5_
  98.2 0.0 collective-permute-done.18.refs_5_.refs_7_
  98.2 5.4 %collective-permute-done.15.refs_2_.refs_4_ = bf16[8,2,128,128]{3,2,1,0:T(8,128)(2,1)S(1)} collective-permute-done((bf16[8,2,128,128]{3,2,1,0:T(8,128)(2,1)}, bf16[8,2,128,128]{3,2,1,0:T(8,128)(2,1)S(1)}, u32[]{:S(2)}, u32[]{:S(2)}) %collective-permute-start.15) | collective-permute-done | bytes 524320 | tf_op jit(solution)/shard_map/ppermute | solution.py:60
  103.6 4.8 %collective-permute-done.17.refs_4_.refs_6_ = bf16[8,2,128,128]{3,2,1,0:T(8,128)(2,1)} collective-permute-done((bf16[8,2,128,128]{3,2,1,0:T(8,128)(2,1)}, bf16[8,2,128,128]{3,2,1,0:T(8,128)(2,1)}, u32[]{:S(2)}, u32[]{:S(2)}) %collective-permute-start.17) | collective-permute-done | bytes 524320 | tf_op jit(solution)/shard_map/ppermute | solution.py:60
  108.4 3.2 %fold.1 = (bf16[64,2,16,128]{3,2,1,0:T(8,128)(2,1)}, bf16[64,2,16,128]{3,2,1,0:T(8,128)(2,1)}) custom-call(s32[2]{0:T(128)} %pad_add_fusion.even, bf16[8,2,64,128]{3,2,1,0:T(8,128)(2,1)} %get-tuple-element.84.refs_0_, bf16[8,2,64,128]{3,2,1,0:T(8,128)(2,1)} %get-tuple-element.85.refs_1_, bf16[8,2,64,128]{3,2,1,0:T(8,128)(2,1)} %get-tuple-element.86.refs_2_, ...), custom_call_target="tpu_custom_call" | custom-call | tf_op jit(solution)/shard_map/fold/pallas_call | solution.py:246
  111.7 2.5 %collective-permute-start.19 = (bf16[64,2,16,128]{3,2,1,0:T(8,128)(2,1)}, bf16[64,2,16,128]{3,2,1,0:T(8,128)(2,1)S(1)}, u32[]{:S(2)}, u32[]{:S(2)}) collective-permute-start(bf16[64,2,16,128]{3,2,1,0:T(8,128)(2,1)} %get-tuple-element.88), channel_id=1, source_target_pairs={{0,16},{2,18},{4,20},{6,22},{8,24},{10,26},{12,28},{14,30},{16,0},... | collective-permute-start | bytes 1572872 | tf_op jit(solution)/shard_map/ppermute | solution.py:60
  114.2 3.1 %collective-permute-start.20 = (bf16[64,2,16,128]{3,2,1,0:T(8,128)(2,1)}, bf16[64,2,16,128]{3,2,1,0:T(8,128)(2,1)S(1)}, u32[]{:S(2)}, u32[]{:S(2)}) collective-permute-start(bf16[64,2,16,128]{3,2,1,0:T(8,128)(2,1)} %get-tuple-element.89), channel_id=1, source_target_pairs={{0,0},{2,2},{4,4},{6,6},{8,8},{10,10},{12,12},{14,14},{16,32},{18,... | collective-permute-start | bytes 1572872 | tf_op jit(solution)/shard_map/ppermute | solution.py:60
  117.3 4.6 %to_tokens.1 = (bf16[1,384,16,128]{3,2,1,0:T(8,128)(2,1)}, bf16[1,384,16,128]{3,2,1,0:T(8,128)(2,1)}) custom-call(bf16[8,384,128]{2,1,0:T(8,128)(2,1)} %get-tuple-element.68.refs_0_, bf16[8,384,128]{2,1,0:T(8,128)(2,1)} %get-tuple-element.71.refs_1_, bf16[8,384,128]{2,1,0:T(8,128)(2,1)} %get-tuple-element.72.refs_2_, ...), custom_call_target="tpu_custom_call" | custom-call | tf_op jit(solution)/shard_map/to_tokens/pallas_call | solution.py:208
  121.9 5.7 %premerge.1 = (bf16[1,384,16,128]{3,2,1,0:T(8,128)(2,1)}, bf16[1,384,16,128]{3,2,1,0:T(8,128)(2,1)}) custom-call(s32[2]{0:T(128)} %pad_add_fusion.even, bf16[8,2,384,128]{3,2,1,0:T(8,128)(2,1)} %get-tuple-element.76.refs_0_, bf16[8,2,384,128]{3,2,1,0:T(8,128)(2,1)} %get-tuple-element.77.refs_1_, bf16[8,2,128,128]{3,2,1,0:T(8,128)(2,1)} %copy-done.5, ...), custom_call_target="tpu_custom_call" | custom-call | tf_op jit(solution)/shard_map/premerge/pallas_call | solution.py:280
  127.6 4.6 %collective-permute-done.19.from_a = bf16[64,2,16,128]{3,2,1,0:T(8,128)(2,1)S(1)} collective-permute-done((bf16[64,2,16,128]{3,2,1,0:T(8,128)(2,1)}, bf16[64,2,16,128]{3,2,1,0:T(8,128)(2,1)S(1)}, u32[]{:S(2)}, u32[]{:S(2)}) %collective-permute-start.19) | collective-permute-done | bytes 524320 | tf_op jit(solution)/shard_map/ppermute | solution.py:60
  132.2 0.0 collective-permute-done.20.from_b
  132.2 0.8 copy-done.8
  133.0 0.2 copy-done.9
  133.2 3.2 %finish.1 = (bf16[1,384,16,128]{3,2,1,0:T(8,128)(2,1)}, bf16[1,384,16,128]{3,2,1,0:T(8,128)(2,1)}) custom-call(s32[2]{0:T(128)} %pad_add_fusion.even, bf16[1,384,16,128]{3,2,1,0:T(8,128)(2,1)} %get-tuple-element.82.dk, bf16[1,384,16,128]{3,2,1,0:T(8,128)(2,1)} %get-tuple-element.83.dv, ...), custom_call_target="tpu_custom_call", output_to_operand_aliasing={{0}: (1, {}), {1}: (2, {})} | custom-call | tf_op jit(solution)/shard_map/finish/pallas_call | solution.py:303
  (32 shorter events, 0.1 us)
Async XLA Ops:
  1.4 7.3 %collective-permute-start.2 = (bf16[4,2,16,128]{3,2,1,0:T(8,128)(2,1)S(1)}, bf16[4,2,16,128]{3,2,1,0:T(8,128)(2,1)S(1)}, u32[]{:S(2)}, u32[]{:S(2)}) collective-permute-start(bf16[4,2,16,128]{3,2,1,0:T(8,128)(2,1)S(1)} %pad_maximum_fusion.4), channel_id=1, source_target_pairs={{0,24},{2,26},{4,28},{6,30},{8,16},{10,18},{12,20},{14,22},{16,8},... | collective-permute-start | bytes 98312 | tf_op jit(solution)/shard_map/ppermute | solution.py:68
  3.6 5.4 %collective-permute-start.1 = (bf16[4,2,16,128]{3,2,1,0:T(8,128)(2,1)S(1)}, bf16[4,2,16,128]{3,2,1,0:T(8,128)(2,1)S(1)}, u32[]{:S(2)}, u32[]{:S(2)}) collective-permute-start(bf16[4,2,16,128]{3,2,1,0:T(8,128)(2,1)S(1)} %pad_maximum_fusion.4), channel_id=1, source_target_pairs={{0,16},{2,18},{4,20},{6,22},{8,24},{10,26},{12,28},{14,30},{16,0},... | collective-permute-start | bytes 98312 | tf_op jit(solution)/shard_map/ppermute | solution.py:68
  4.3 4.7 %collective-permute-start = (bf16[4,2,16,128]{3,2,1,0:T(8,128)(2,1)S(1)}, bf16[4,2,16,128]{3,2,1,0:T(8,128)(2,1)S(1)}, u32[]{:S(2)}, u32[]{:S(2)}) collective-permute-start(bf16[4,2,16,128]{3,2,1,0:T(8,128)(2,1)S(1)} %pad_maximum_fusion.4), channel_id=1, source_target_pairs={{0,8},{2,10},{4,12},{6,14},{8,0},{10,2},{12,4},{14,6},{16,24},{18,... | collective-permute-start | bytes 98312 | tf_op jit(solution)/shard_map/ppermute | solution.py:68
  7.0 2.1 %copy-start.10 = (bf16[1,4,16,128]{3,2,1,0:T(8,128)(2,1)S(1)}, bf16[1,4,16,128]{3,2,1,0:T(8,128)(2,1)}, u32[]{:S(2)}) copy-start(bf16[1,4,16,128]{3,2,1,0:T(8,128)(2,1)} %param.10) | copy-start | bytes 49156
  7.0 2.0 %copy-start.11 = (bf16[1,4,16,128]{3,2,1,0:T(8,128)(2,1)S(1)}, bf16[1,4,16,128]{3,2,1,0:T(8,128)(2,1)}, u32[]{:S(2)}) copy-start(bf16[1,4,16,128]{3,2,1,0:T(8,128)(2,1)} %param.9) | copy-start | bytes 49156
  9.0 12.0 %collective-permute-start.7 = (bf16[16,2,16,128]{3,2,1,0:T(8,128)(2,1)S(1)}, bf16[16,2,16,128]{3,2,1,0:T(8,128)(2,1)S(1)}, u32[]{:S(2)}, u32[]{:S(2)}) collective-permute-start(bf16[16,2,16,128]{3,2,1,0:T(8,128)(2,1)S(1)} %pad_maximum_fusion.3), channel_id=1, source_target_pairs={{0,96},{2,98},{4,100},{6,102},{8,104},{10,106},{12,108},{14,110},{... | collective-permute-start | bytes 393224 | tf_op jit(solution)/shard_map/ppermute | solution.py:68
  13.5 9.7 %collective-permute-start.6 = (bf16[16,2,16,128]{3,2,1,0:T(8,128)(2,1)S(1)}, bf16[16,2,16,128]{3,2,1,0:T(8,128)(2,1)S(1)}, u32[]{:S(2)}, u32[]{:S(2)}) collective-permute-start(bf16[16,2,16,128]{3,2,1,0:T(8,128)(2,1)S(1)} %pad_maximum_fusion.3), channel_id=1, source_target_pairs={{0,64},{2,66},{4,68},{6,70},{8,72},{10,74},{12,76},{14,78},{16,80}... | collective-permute-start | bytes 393224 | tf_op jit(solution)/shard_map/ppermute | solution.py:68
  13.5 9.7 %collective-permute-start.5 = (bf16[16,2,16,128]{3,2,1,0:T(8,128)(2,1)S(1)}, bf16[16,2,16,128]{3,2,1,0:T(8,128)(2,1)S(1)}, u32[]{:S(2)}, u32[]{:S(2)}) collective-permute-start(bf16[16,2,16,128]{3,2,1,0:T(8,128)(2,1)S(1)} %pad_maximum_fusion.3), channel_id=1, source_target_pairs={{0,32},{2,34},{4,36},{6,38},{8,40},{10,42},{12,44},{14,46},{16,48}... | collective-permute-start | bytes 393224 | tf_op jit(solution)/shard_map/ppermute | solution.py:68
  14.1 25.2 %collective-permute-start.3 = (bf16[64,2,16,128]{3,2,1,0:T(8,128)(2,1)}, bf16[64,2,16,128]{3,2,1,0:T(8,128)(2,1)S(1)}, u32[]{:S(2)}, u32[]{:S(2)}) collective-permute-start(bf16[64,2,16,128]{3,2,1,0:T(8,128)(2,1)} %pad_maximum_fusion), channel_id=1, source_target_pairs={{0,16},{2,18},{4,20},{6,22},{8,24},{10,26},{12,28},{14,30},{16,0},... | collective-permute-start | bytes 1572872 | tf_op jit(solution)/shard_map/ppermute | solution.py:60
  15.5 23.8 %collective-permute-start.4 = (bf16[64,2,16,128]{3,2,1,0:T(8,128)(2,1)}, bf16[64,2,16,128]{3,2,1,0:T(8,128)(2,1)S(1)}, u32[]{:S(2)}, u32[]{:S(2)}) collective-permute-start(bf16[64,2,16,128]{3,2,1,0:T(8,128)(2,1)} %pad_maximum_fusion.1), channel_id=1, source_target_pairs={{0,0},{2,2},{4,4},{6,6},{8,8},{10,10},{12,12},{14,14},{16,32},{18,... | collective-permute-start | bytes 1572872 | tf_op jit(solution)/shard_map/ppermute | solution.py:60
  23.3 10.1 %copy-start = (bf16[64,2,16,128]{3,2,1,0:T(8,128)(2,1)}, bf16[64,2,16,128]{3,2,1,0:T(8,128)(2,1)S(1)}, u32[]{:S(2)}) copy-start(bf16[64,2,16,128]{3,2,1,0:T(8,128)(2,1)S(1)} %pad_maximum_fusion.2.refs_0_) | copy-start | bytes 1572868
  23.3 27.0 %collective-permute-start.10 = (bf16[64,2,16,128]{3,2,1,0:T(8,128)(2,1)S(1)}, bf16[64,2,16,128]{3,2,1,0:T(8,128)(2,1)}, u32[]{:S(2)}, u32[]{:S(2)}) collective-permute-start(bf16[64,2,16,128]{3,2,1,0:T(8,128)(2,1)S(1)} %pad_maximum_fusion.2.refs_0_), channel_id=1, source_target_pairs={{0,6},{2,4},{4,2},{6,0},{8,14},{10,12},{12,10},{14,8},{16,22},{18,... | collective-permute-start | bytes 1572872 | tf_op jit(solution)/shard_map/ppermute | solution.py:68
  26.4 24.4 %collective-permute-start.9 = (bf16[64,2,16,128]{3,2,1,0:T(8,128)(2,1)S(1)}, bf16[64,2,16,128]{3,2,1,0:T(8,128)(2,1)}, u32[]{:S(2)}, u32[]{:S(2)}) collective-permute-start(bf16[64,2,16,128]{3,2,1,0:T(8,128)(2,1)S(1)} %pad_maximum_fusion.2.refs_0_), channel_id=1, source_target_pairs={{0,4},{2,6},{4,0},{6,2},{8,12},{10,14},{12,8},{14,10},{16,20},{18,... | collective-permute-start | bytes 1572872 | tf_op jit(solution)/shard_map/ppermute | solution.py:68
  28.1 28.5 %collective-permute-start.8 = (bf16[64,2,16,128]{3,2,1,0:T(8,128)(2,1)S(1)}, bf16[64,2,16,128]{3,2,1,0:T(8,128)(2,1)}, u32[]{:S(2)}, u32[]{:S(2)}) collective-permute-start(bf16[64,2,16,128]{3,2,1,0:T(8,128)(2,1)S(1)} %pad_maximum_fusion.2.refs_0_), channel_id=1, source_target_pairs={{0,2},{2,0},{4,6},{6,4},{8,10},{10,8},{12,14},{14,12},{16,18},{18,... | collective-permute-start | bytes 1572872 | tf_op jit(solution)/shard_map/ppermute | solution.py:68
  39.3 0.8 copy-start.1
  39.4 1.0 copy-start.2
  44.4 18.4 %collective-permute-start.13 = (bf16[128,2,8,128]{3,2,1,0:T(8,128)(2,1)}, bf16[128,2,8,128]{3,2,1,0:T(8,128)(2,1)S(1)}, u32[]{:S(2)}, u32[]{:S(2)}) collective-permute-start(bf16[128,2,8,128]{3,2,1,0:T(8,128)(2,1)} %get-tuple-element.69), channel_id=1, source_target_pairs={{0,2},{2,0},{4,6},{6,4},{8,10},{10,8},{12,14},{14,12},{16,18},{18,... | collective-permute-start | bytes 1572872 | tf_op jit(solution)/shard_map/ppermute | solution.py:60
  45.9 19.2 %collective-permute-start.14 = (bf16[128,2,8,128]{3,2,1,0:T(8,128)(2,1)}, bf16[128,2,8,128]{3,2,1,0:T(8,128)(2,1)}, u32[]{:S(2)}, u32[]{:S(2)}) collective-permute-start(bf16[128,2,8,128]{3,2,1,0:T(8,128)(2,1)} %get-tuple-element.70), channel_id=1, source_target_pairs={{0,0},{2,4},{4,2},{6,8},{8,6},{10,12},{12,10},{14,14},{16,16},{18,... | collective-permute-start | bytes 1572872 | tf_op jit(solution)/shard_map/ppermute | solution.py:60
  50.3 31.2 %collective-permute-start.11 = (bf16[128,2,8,128]{3,2,1,0:T(8,128)(2,1)}, bf16[128,2,8,128]{3,2,1,0:T(8,128)(2,1)S(1)}, u32[]{:S(2)}, u32[]{:S(2)}) collective-permute-start(bf16[128,2,8,128]{3,2,1,0:T(8,128)(2,1)} %get-tuple-element.65), channel_id=1, source_target_pairs={{0,2},{2,0},{4,6},{6,4},{8,10},{10,8},{12,14},{14,12},{16,18},{18,... | collective-permute-start | bytes 1572872 | tf_op jit(solution)/shard_map/ppermute | solution.py:60
  50.8 30.7 %collective-permute-start.12 = (bf16[128,2,8,128]{3,2,1,0:T(8,128)(2,1)}, bf16[128,2,8,128]{3,2,1,0:T(8,128)(2,1)}, u32[]{:S(2)}, u32[]{:S(2)}) collective-permute-start(bf16[128,2,8,128]{3,2,1,0:T(8,128)(2,1)} %get-tuple-element.66), channel_id=1, source_target_pairs={{0,0},{2,4},{4,2},{6,8},{8,6},{10,12},{12,10},{14,14},{16,16},{18,... | collective-permute-start | bytes 1572872 | tf_op jit(solution)/shard_map/ppermute | solution.py:60
  62.8 2.3 %copy-start.7 = (bf16[128,2,8,128]{3,2,1,0:T(8,128)(2,1)}, bf16[128,2,8,128]{3,2,1,0:T(8,128)(2,1)S(1)}, u32[]{:S(2)}) copy-start(bf16[128,2,8,128]{3,2,1,0:T(8,128)(2,1)S(1)} %collective-permute-done.13.sa) | copy-start | bytes 1572868
  77.0 21.1 %collective-permute-start.16 = (bf16[8,2,128,128]{3,2,1,0:T(8,128)(2,1)}, bf16[8,2,128,128]{3,2,1,0:T(8,128)(2,1)S(1)}, u32[]{:S(2)}, u32[]{:S(2)}) collective-permute-start(bf16[8,2,128,128]{3,2,1,0:T(8,128)(2,1)} %get-tuple-element.79), channel_id=1, source_target_pairs={{0,2},{2,0},{4,6},{6,4},{8,10},{10,8},{12,14},{14,12},{16,18},{18,... | collective-permute-start | bytes 1572872 | tf_op jit(solution)/shard_map/ppermute | solution.py:60
  77.1 21.1 %collective-permute-start.18 = (bf16[8,2,128,128]{3,2,1,0:T(8,128)(2,1)}, bf16[8,2,128,128]{3,2,1,0:T(8,128)(2,1)S(1)}, u32[]{:S(2)}, u32[]{:S(2)}) collective-permute-start(bf16[8,2,128,128]{3,2,1,0:T(8,128)(2,1)} %get-tuple-element.81), channel_id=1, source_target_pairs={{0,0},{2,4},{4,2},{6,8},{8,6},{10,12},{12,10},{14,14},{16,16},{18,... | collective-permute-start | bytes 1572872 | tf_op jit(solution)/shard_map/ppermute | solution.py:60
  81.5 0.8 copy-start.6
  94.1 9.5 %collective-permute-start.15 = (bf16[8,2,128,128]{3,2,1,0:T(8,128)(2,1)}, bf16[8,2,128,128]{3,2,1,0:T(8,128)(2,1)S(1)}, u32[]{:S(2)}, u32[]{:S(2)}) collective-permute-start(bf16[8,2,128,128]{3,2,1,0:T(8,128)(2,1)} %get-tuple-element.78), channel_id=1, source_target_pairs={{0,2},{2,0},{4,6},{6,4},{8,10},{10,8},{12,14},{14,12},{16,18},{18,... | collective-permute-start | bytes 1572872 | tf_op jit(solution)/shard_map/ppermute | solution.py:60
  94.6 13.8 %collective-permute-start.17 = (bf16[8,2,128,128]{3,2,1,0:T(8,128)(2,1)}, bf16[8,2,128,128]{3,2,1,0:T(8,128)(2,1)}, u32[]{:S(2)}, u32[]{:S(2)}) collective-permute-start(bf16[8,2,128,128]{3,2,1,0:T(8,128)(2,1)} %get-tuple-element.80), channel_id=1, source_target_pairs={{0,0},{2,4},{4,2},{6,8},{8,6},{10,12},{12,10},{14,14},{16,16},{18,... | collective-permute-start | bytes 1572872 | tf_op jit(solution)/shard_map/ppermute | solution.py:60
  98.2 10.3 %copy-start.3 = (bf16[8,2,128,128]{3,2,1,0:T(8,128)(2,1)}, bf16[8,2,128,128]{3,2,1,0:T(8,128)(2,1)S(1)}, u32[]{:S(2)}) copy-start(bf16[8,2,128,128]{3,2,1,0:T(8,128)(2,1)S(1)} %collective-permute-done.16.refs_3_.refs_5_) | copy-start | bytes 1572868
  98.2 10.3 %copy-start.4 = (bf16[8,2,128,128]{3,2,1,0:T(8,128)(2,1)}, bf16[8,2,128,128]{3,2,1,0:T(8,128)(2,1)S(1)}, u32[]{:S(2)}) copy-start(bf16[8,2,128,128]{3,2,1,0:T(8,128)(2,1)S(1)} %collective-permute-done.18.refs_5_.refs_7_) | copy-start | bytes 1572868
  103.6 4.8 %copy-start.5 = (bf16[8,2,128,128]{3,2,1,0:T(8,128)(2,1)}, bf16[8,2,128,128]{3,2,1,0:T(8,128)(2,1)S(1)}, u32[]{:S(2)}) copy-start(bf16[8,2,128,128]{3,2,1,0:T(8,128)(2,1)S(1)} %collective-permute-done.15.refs_2_.refs_4_) | copy-start | bytes 1572868
  111.7 20.5 %collective-permute-start.19 = (bf16[64,2,16,128]{3,2,1,0:T(8,128)(2,1)}, bf16[64,2,16,128]{3,2,1,0:T(8,128)(2,1)S(1)}, u32[]{:S(2)}, u32[]{:S(2)}) collective-permute-start(bf16[64,2,16,128]{3,2,1,0:T(8,128)(2,1)} %get-tuple-element.88), channel_id=1, source_target_pairs={{0,16},{2,18},{4,20},{6,22},{8,24},{10,26},{12,28},{14,30},{16,0},... | collective-permute-start | bytes 1572872 | tf_op jit(solution)/shard_map/ppermute | solution.py:60
  114.2 18.0 %collective-permute-start.20 = (bf16[64,2,16,128]{3,2,1,0:T(8,128)(2,1)}, bf16[64,2,16,128]{3,2,1,0:T(8,128)(2,1)S(1)}, u32[]{:S(2)}, u32[]{:S(2)}) collective-permute-start(bf16[64,2,16,128]{3,2,1,0:T(8,128)(2,1)} %get-tuple-element.89), channel_id=1, source_target_pairs={{0,0},{2,2},{4,4},{6,6},{8,8},{10,10},{12,12},{14,14},{16,32},{18,... | collective-permute-start | bytes 1572872 | tf_op jit(solution)/shard_map/ppermute | solution.py:60
  132.2 0.8 copy-start.8
  132.2 1.0 copy-start.9

commit v2 on v1

--- a/solution.py
+++ b/solution.py
@@ -28,7 +28,7 @@
 F32 = jnp.float32
 SMEM = pl.BlockSpec(memory_space=pltpu.SMEM)
 VMEM = pl.BlockSpec(memory_space=pltpu.VMEM)
-PARAMS = pltpu.CompilerParams(vmem_limit_bytes=62 << 20)
+PARAMS = pltpu.CompilerParams(vmem_limit_bytes=56 << 20)
 
 
 def nt(a, b):

time: 138 us -> 137 us (level)
  waiting for transfers between devices: 24.1 us -> 20.6 us
  local copies, waits for them, and re-layouts: 4.12 us -> 7.39 us
  other arithmetic: 4.33 us -> 2.74 us
  starting transfers between devices: 43.4 us -> 44.8 us
    ppermute x12, waiting for transfers between devices: 21.6 us -> 16.9 us  [exchange(): return lax.ppermute(value, 'seq', pairs)]
    unnamed x24 -> x36, local copies, waits for them, and re-layouts: 2.74 us -> 6.01 us
    ppermute x12, starting transfers between devices: 30.1 us -> 32 us  [exchange(): return lax.ppermute(value, 'seq', pairs)]
    another operation x2, other arithmetic: 1.7 us -> 0.1 us  [shards(): jnp.stack([lax.dynamic_slice_in_dim(x[0], o, EDGE, 0) for x in (fine_keys...]
  transfers between devices with their start and end apart: 21 -> 21, of which waited for: 8 -> 9; matrix products, arithmetic and copies ran while one was open for 4% -> 2% of each run, Pallas kernels for 39% -> 39%
where the time goes in v2:
time: 137 us; the launch traced here: 136 us
  Pallas kernels  59.4 us (43%)
  starting transfers between devices  44.8 us (33%)
  waiting for transfers between devices  20.6 us (15%)
  local copies, waits for them, and re-layouts  7.39 us (5%)
  other arithmetic  2.74 us (2%)
    ppermute x12, starting transfers between devices, exchange(): return lax.ppermute(value, 'seq', pairs)  32 us
    pallas_call x2, Pallas kernels, attend(): pl.pallas_call(functools.partial(attend_kernel, heads), grid=(steps,), in...  23.7 us
    ppermute x12, waiting for transfers between devices, exchange(): return lax.ppermute(value, 'seq', pairs)  16.9 us
    ppermute x9, starting transfers between devices, swapped(): return lax.ppermute(block, 'seq', pairs)  12.8 us
    unnamed x36, local copies, waits for them, and re-layouts  6.01 us
    pallas_call x1, Pallas kernels, premerge(): pl.pallas_call(premerge_kernel, in_specs=[SMEM] + [VMEM] * (3 * CHUNKS),...  5.65 us
    pallas_call x1, Pallas kernels, pairs_to_heads(): pl.pallas_call(pairs_to_heads_kernel, grid=(BLOCKS,), in_specs=[tokens, t...  4.84 us
    pallas_call x1, Pallas kernels, to_heads(): pl.pallas_call(to_heads_kernel, grid=(BLOCKS,), in_specs=[tokens, tokens]...  4.81 us
  transfers between devices with their start and end apart: 21, of which 9 were waited for; matrix products, arithmetic and copies ran while one was open for 2% of the time, Pallas kernels for 39%

profile of v2, /device:TPU:6, one launch (start us, length us, event | category | flops | bytes accessed | tf_op | source)
XLA Modules:
  0.0 136.0 jit_solution(1386253696392968792)
XLA Ops:
  0.6 0.7 pad_maximum_fusion.4
  1.4 2.2 %collective-permute-start.2 = (bf16[4,2,16,128]{3,2,1,0:T(8,128)(2,1)S(1)}, bf16[4,2,16,128]{3,2,1,0:T(8,128)(2,1)S(1)}, u32[]{:S(2)}, u32[]{:S(2)}) collective-permute-start(bf16[4,2,16,128]{3,2,1,0:T(8,128)(2,1)S(1)} %pad_maximum_fusion.4), channel_id=1, source_target_pairs={{0,24},{2,26},{4,28},{6,30},{8,16},{10,18},{12,20},{14,22},{16,8},... | collective-permute-start | bytes 98312 | tf_op jit(solution)/shard_map/ppermute | solution.py:68
  3.6 0.7 collective-permute-start.1
  4.3 1.2 collective-permute-start
  5.6 1.4 %dynamic-slice_bitcast_fusion = (bf16[64,1,16,128]{3,2,1,0:T(8,128)(2,1)S(1)}, bf16[64,1,16,128]{3,2,1,0:T(8,128)(2,1)S(1)}, bf16[64,1,16,128]{3,2,1,0:T(8,128)(2,1)S(1)}, bf16[64,1,16,128]{3,2,1,0:T(8,128)(2,1)S(1)}) fusion(bf16[1,384,16,128]{3,2,1,0:T(8,128)(2,1)} %v, s32[]{:T(128)S(6)} %select_n.93, s32[]{:T(128)S(6)} %select_n.92, ...), kind=kLoop, calls=%fused_computation.31 | loop fusion | bytes 2097160 | tf_op jit(solution)/shard_map/stack | solution.py:451
  7.0 0.0 copy-start.16
  7.0 0.0 copy-start.17
  7.1 1.9 %collective-permute-done.1 = bf16[4,2,16,128]{3,2,1,0:T(8,128)(2,1)S(1)} collective-permute-done((bf16[4,2,16,128]{3,2,1,0:T(8,128)(2,1)S(1)}, bf16[4,2,16,128]{3,2,1,0:T(8,128)(2,1)S(1)}, u32[]{:S(2)}, u32[]{:S(2)}) %collective-permute-start.1) | collective-permute-done | bytes 32800 | tf_op jit(solution)/shard_map/ppermute | solution.py:68
  9.0 0.0 collective-permute-done
  9.0 3.9 %collective-permute-start.7 = (bf16[16,2,16,128]{3,2,1,0:T(8,128)(2,1)S(1)}, bf16[16,2,16,128]{3,2,1,0:T(8,128)(2,1)S(1)}, u32[]{:S(2)}, u32[]{:S(2)}) collective-permute-start(bf16[16,2,16,128]{3,2,1,0:T(8,128)(2,1)S(1)} %pad_maximum_fusion.3), channel_id=1, source_target_pairs={{0,96},{2,98},{4,100},{6,102},{8,104},{10,106},{12,108},{14,110},{... | collective-permute-start | bytes 393224 | tf_op jit(solution)/shard_map/ppermute | solution.py:68
  12.9 0.0 collective-permute-start.6
  12.9 0.7 collective-permute-start.5
  13.6 1.9 %collective-permute-start.3 = (bf16[64,2,16,128]{3,2,1,0:T(8,128)(2,1)S(1)}, bf16[64,2,16,128]{3,2,1,0:T(8,128)(2,1)S(1)}, u32[]{:S(2)}, u32[]{:S(2)}) collective-permute-start(bf16[64,2,16,128]{3,2,1,0:T(8,128)(2,1)S(1)} %pad_maximum_fusion), channel_id=1, source_target_pairs={{0,16},{2,18},{4,20},{6,22},{8,24},{10,26},{12,28},{14,30},{16,0},... | collective-permute-start | bytes 1572872 | tf_op jit(solution)/shard_map/ppermute | solution.py:60
  15.5 4.3 %collective-permute-start.4 = (bf16[64,2,16,128]{3,2,1,0:T(8,128)(2,1)S(1)}, bf16[64,2,16,128]{3,2,1,0:T(8,128)(2,1)S(1)}, u32[]{:S(2)}, u32[]{:S(2)}) collective-permute-start(bf16[64,2,16,128]{3,2,1,0:T(8,128)(2,1)S(1)} %pad_maximum_fusion.1), channel_id=1, source_target_pairs={{0,0},{2,2},{4,4},{6,6},{8,8},{10,10},{12,12},{14,14},{16,32},{18,... | collective-permute-start | bytes 1572872 | tf_op jit(solution)/shard_map/ppermute | solution.py:60
  19.8 0.7 pad_add_fusion.even
  20.5 0.0 collective-permute-done.7
  20.5 1.7 %collective-permute-done.6 = bf16[16,2,16,128]{3,2,1,0:T(8,128)(2,1)S(1)} collective-permute-done((bf16[16,2,16,128]{3,2,1,0:T(8,128)(2,1)S(1)}, bf16[16,2,16,128]{3,2,1,0:T(8,128)(2,1)S(1)}, u32[]{:S(2)}, u32[]{:S(2)}) %collective-permute-start.6) | collective-permute-done | bytes 131104 | tf_op jit(solution)/shard_map/ppermute | solution.py:68
  22.2 0.2 collective-permute-done.5
  22.4 0.1 pad_maximum_fusion.2.refs_0_
  22.4 3.1 %collective-permute-start.10 = (bf16[64,2,16,128]{3,2,1,0:T(8,128)(2,1)S(1)}, bf16[64,2,16,128]{3,2,1,0:T(8,128)(2,1)S(1)}, u32[]{:S(2)}, u32[]{:S(2)}) collective-permute-start(bf16[64,2,16,128]{3,2,1,0:T(8,128)(2,1)S(1)} %pad_maximum_fusion.2.refs_0_), channel_id=1, source_target_pairs={{0,6},{2,4},{4,2},{6,0},{8,14},{10,12},{12,10},{14,8},{16,22},{18,... | collective-permute-start | bytes 1572872 | tf_op jit(solution)/shard_map/ppermute | solution.py:68
  25.5 0.6 collective-permute-start.9
  26.2 1.1 fusion.16.bias
  27.2 0.5 collective-permute-start.8
  27.7 4.8 %pairs_to_heads.1.kv = bf16[16,2,384,128]{3,2,1,0:T(8,128)(2,1)} custom-call(bf16[1,384,16,128]{3,2,1,0:T(8,128)(2,1)} %k, bf16[1,384,16,128]{3,2,1,0:T(8,128)(2,1)} %v), custom_call_target="tpu_custom_call" | custom-call | tf_op jit(solution)/shard_map/pairs_to_heads/pallas_call | solution.py:82
  32.5 4.8 %to_heads.1 = (bf16[16,384,128]{2,1,0:T(8,128)(2,1)}, bf16[16,384,128]{2,1,0:T(8,128)(2,1)}) custom-call(bf16[1,384,16,128]{3,2,1,0:T(8,128)(2,1)} %x, bf16[1,384,16,128]{3,2,1,0:T(8,128)(2,1)} %y), custom_call_target="tpu_custom_call" | custom-call | tf_op jit(solution)/shard_map/to_heads/pallas_call | solution.py:103
  37.3 0.8 collective-permute-done.3.x.a
  38.1 0.0 collective-permute-done.4.y.b
  38.1 0.8 copy-done.1
  38.9 0.2 copy-done.2
  39.1 4.1 %sides.1 = (bf16[128,2,8,128]{3,2,1,0:T(8,128)(2,1)}, bf16[128,2,8,128]{3,2,1,0:T(8,128)(2,1)}, bf16[128,2,8,128]{3,2,1,0:T(8,128)(2,1)}, bf16[128,2,8,128]{3,2,1,0:T(8,128)(2,1)}) custom-call(s32[2]{0:T(128)} %pad_add_fusion.even, bf16[64,2,16,128]{3,2,1,0:T(8,128)(2,1)} %copy-done.1, bf16[64,2,16,128]{3,2,1,0:T(8,128)(2,1)} %copy-done.2, ...), custom_call_target="tpu_custom_call" | custom-call | tf_op jit(solution)/shard_map/sides/pallas_call | solution.py:183
  43.1 1.6 %collective-permute-start.13 = (bf16[128,2,8,128]{3,2,1,0:T(8,128)(2,1)}, bf16[128,2,8,128]{3,2,1,0:T(8,128)(2,1)S(1)}, u32[]{:S(2)}, u32[]{:S(2)}) collective-permute-start(bf16[128,2,8,128]{3,2,1,0:T(8,128)(2,1)} %get-tuple-element.69), channel_id=1, source_target_pairs={{0,2},{2,0},{4,6},{6,4},{8,10},{10,8},{12,14},{14,12},{16,18},{18,... | collective-permute-start | bytes 1572872 | tf_op jit(solution)/shard_map/ppermute | solution.py:60
  44.7 4.3 %collective-permute-start.14 = (bf16[128,2,8,128]{3,2,1,0:T(8,128)(2,1)}, bf16[128,2,8,128]{3,2,1,0:T(8,128)(2,1)S(1)}, u32[]{:S(2)}, u32[]{:S(2)}) collective-permute-start(bf16[128,2,8,128]{3,2,1,0:T(8,128)(2,1)} %get-tuple-element.70), channel_id=1, source_target_pairs={{0,0},{2,4},{4,2},{6,8},{8,6},{10,12},{12,10},{14,14},{16,16},{18,... | collective-permute-start | bytes 1572872 | tf_op jit(solution)/shard_map/ppermute | solution.py:60
  49.1 0.5 collective-permute-start.11
  49.6 3.4 %collective-permute-start.12 = (bf16[128,2,8,128]{3,2,1,0:T(8,128)(2,1)}, bf16[128,2,8,128]{3,2,1,0:T(8,128)(2,1)S(1)}, u32[]{:S(2)}, u32[]{:S(2)}) collective-permute-start(bf16[128,2,8,128]{3,2,1,0:T(8,128)(2,1)} %get-tuple-element.66), channel_id=1, source_target_pairs={{0,0},{2,4},{4,2},{6,8},{8,6},{10,12},{12,10},{14,14},{16,16},{18,... | collective-permute-start | bytes 1572872 | tf_op jit(solution)/shard_map/ppermute | solution.py:60
  53.0 2.4 %halo_to_heads.1 = (bf16[16,2,64,128]{3,2,1,0:T(8,128)(2,1)}, bf16[16,2,64,128]{3,2,1,0:T(8,128)(2,1)}) custom-call(s32[2]{0:T(128)} %pad_add_fusion.even, bf16[64,2,16,128]{3,2,1,0:T(8,128)(2,1)} %copy-done.1, bf16[64,2,16,128]{3,2,1,0:T(8,128)(2,1)} %copy-done.2), custom_call_target="tpu_custom_call" | custom-call | tf_op jit(solution)/shard_map/halo_to_heads/pallas_call | solution.py:125
  55.4 0.0 collective-permute-done.8.refs_1_
  55.4 0.0 copy-start.15
  55.4 0.8 copy-done.15
  56.2 2.9 %far_heads.1.far = bf16[16,2,256,128]{3,2,1,0:T(8,128)(2,1)} custom-call(bf16[64,2,16,128]{3,2,1,0:T(8,128)(2,1)} %copy-done, bf16[64,2,16,128]{3,2,1,0:T(8,128)(2,1)} %copy-done.15, bf16[64,2,16,128]{3,2,1,0:T(8,128)(2,1)} %copy-done.14, bf16[64,2,16,128]{3,2,1,0:T(8,128)(2,1)} %copy-done.13), custom_call_target="tpu_custom_call" | custom-call | tf_op jit(solution)/shard_map/far_heads/pallas_call | solution.py:146
  59.1 2.9 %collective-permute-done.13.sa = bf16[128,2,8,128]{3,2,1,0:T(8,128)(2,1)S(1)} collective-permute-done((bf16[128,2,8,128]{3,2,1,0:T(8,128)(2,1)}, bf16[128,2,8,128]{3,2,1,0:T(8,128)(2,1)S(1)}, u32[]{:S(2)}, u32[]{:S(2)}) %collective-permute-start.13) | collective-permute-done | bytes 524320 | tf_op jit(solution)/shard_map/ppermute | solution.py:60
  61.9 1.8 %collective-permute-done.14.sb = bf16[128,2,8,128]{3,2,1,0:T(8,128)(2,1)S(1)} collective-permute-done((bf16[128,2,8,128]{3,2,1,0:T(8,128)(2,1)}, bf16[128,2,8,128]{3,2,1,0:T(8,128)(2,1)S(1)}, u32[]{:S(2)}, u32[]{:S(2)}) %collective-permute-start.14) | collective-permute-done | bytes 524320 | tf_op jit(solution)/shard_map/ppermute | solution.py:60
  63.8 0.9 copy-done.10
  64.6 11.9 %attend.3 = (bf16[8,384,128]{2,1,0:T(8,128)(2,1)}, bf16[8,384,128]{2,1,0:T(8,128)(2,1)}, bf16[8,2,384,128]{3,2,1,0:T(8,128)(2,1)}, bf16[8,2,64,128]{3,2,1,0:T(8,...) custom-call(bf16[16,384,128]{2,1,0:T(8,128)(2,1)} %get-tuple-element., ...), custom_call_target="tpu_custom_call" | custom-call | flops 2617245696 | bytes 12582912 | tf_op jit(solution)/shard_map/attend/pallas_call | solution.py:413
  76.5 0.1 collective-permute-start.16
  76.6 4.3 %collective-permute-start.18 = (bf16[8,2,128,128]{3,2,1,0:T(8,128)(2,1)}, bf16[8,2,128,128]{3,2,1,0:T(8,128)(2,1)S(1)}, u32[]{:S(2)}, u32[]{:S(2)}) collective-permute-start(bf16[8,2,128,128]{3,2,1,0:T(8,128)(2,1)} %get-tuple-element.81), channel_id=1, source_target_pairs={{0,0},{2,4},{4,2},{6,8},{8,6},{10,12},{12,10},{14,14},{16,16},{18,... | collective-permute-start | bytes 1572872 | tf_op jit(solution)/shard_map/ppermute | solution.py:60
  81.0 0.0 copy-start.7
  81.0 0.0 collective-permute-done.12.sb
  81.0 0.8 copy-done.7
  81.8 0.8 copy-done.8
  82.6 11.8 %attend.2 = (bf16[8,384,128]{2,1,0:T(8,128)(2,1)}, bf16[8,384,128]{2,1,0:T(8,128)(2,1)}, bf16[8,2,384,128]{3,2,1,0:T(8,128)(2,1)}, bf16[8,2,64,128]{3,2,1,0:T(8,...) custom-call(bf16[16,384,128]{2,1,0:T(8,128)(2,1)} %get-tuple-element., ...), custom_call_target="tpu_custom_call" | custom-call | flops 2617245696 | bytes 12582912 | tf_op jit(solution)/shard_map/attend/pallas_call | solution.py:413
  94.4 0.4 collective-permute-start.15
  94.8 3.6 %collective-permute-start.17 = (bf16[8,2,128,128]{3,2,1,0:T(8,128)(2,1)}, bf16[8,2,128,128]{3,2,1,0:T(8,128)(2,1)S(1)}, u32[]{:S(2)}, u32[]{:S(2)}) collective-permute-start(bf16[8,2,128,128]{3,2,1,0:T(8,128)(2,1)} %get-tuple-element.80), channel_id=1, source_target_pairs={{0,0},{2,4},{4,2},{6,8},{8,6},{10,12},{12,10},{14,14},{16,16},{18,... | collective-permute-start | bytes 1572872 | tf_op jit(solution)/shard_map/ppermute | solution.py:60
  98.5 5.4 %collective-permute-done.15.refs_2_.refs_4_ = bf16[8,2,128,128]{3,2,1,0:T(8,128)(2,1)S(1)} collective-permute-done((bf16[8,2,128,128]{3,2,1,0:T(8,128)(2,1)}, bf16[8,2,128,128]{3,2,1,0:T(8,128)(2,1)S(1)}, u32[]{:S(2)}, u32[]{:S(2)}) %collective-permute-start.15) | collective-permute-done | bytes 524320 | tf_op jit(solution)/shard_map/ppermute | solution.py:60
  103.9 4.3 %collective-permute-done.17.refs_4_.refs_6_ = bf16[8,2,128,128]{3,2,1,0:T(8,128)(2,1)S(1)} collective-permute-done((bf16[8,2,128,128]{3,2,1,0:T(8,128)(2,1)}, bf16[8,2,128,128]{3,2,1,0:T(8,128)(2,1)S(1)}, u32[]{:S(2)}, u32[]{:S(2)}) %collective-permute-start.17) | collective-permute-done | bytes 524320 | tf_op jit(solution)/shard_map/ppermute | solution.py:60
  108.2 0.8 copy-done.6
  109.0 3.2 %fold.1 = (bf16[64,2,16,128]{3,2,1,0:T(8,128)(2,1)}, bf16[64,2,16,128]{3,2,1,0:T(8,128)(2,1)}) custom-call(s32[2]{0:T(128)} %pad_add_fusion.even, bf16[8,2,64,128]{3,2,1,0:T(8,128)(2,1)} %get-tuple-element.84.refs_0_, bf16[8,2,64,128]{3,2,1,0:T(8,128)(2,1)} %get-tuple-element.85.refs_1_, bf16[8,2,64,128]{3,2,1,0:T(8,128)(2,1)} %get-tuple-element.86.refs_2_, ...), custom_call_target="tpu_custom_call" | custom-call | tf_op jit(solution)/shard_map/fold/pallas_call | solution.py:246
  112.2 3.2 %collective-permute-start.19 = (bf16[64,2,16,128]{3,2,1,0:T(8,128)(2,1)}, bf16[64,2,16,128]{3,2,1,0:T(8,128)(2,1)S(1)}, u32[]{:S(2)}, u32[]{:S(2)}) collective-permute-start(bf16[64,2,16,128]{3,2,1,0:T(8,128)(2,1)} %get-tuple-element.88), channel_id=1, source_target_pairs={{0,16},{2,18},{4,20},{6,22},{8,24},{10,26},{12,28},{14,30},{16,0},... | collective-permute-start | bytes 1572872 | tf_op jit(solution)/shard_map/ppermute | solution.py:60
  115.5 4.3 %collective-permute-start.20 = (bf16[64,2,16,128]{3,2,1,0:T(8,128)(2,1)}, bf16[64,2,16,128]{3,2,1,0:T(8,128)(2,1)S(1)}, u32[]{:S(2)}, u32[]{:S(2)}) collective-permute-start(bf16[64,2,16,128]{3,2,1,0:T(8,128)(2,1)} %get-tuple-element.89), channel_id=1, source_target_pairs={{0,0},{2,2},{4,4},{6,6},{8,8},{10,10},{12,12},{14,14},{16,32},{18,... | collective-permute-start | bytes 1572872 | tf_op jit(solution)/shard_map/ppermute | solution.py:60
  119.8 4.6 %to_tokens.1 = (bf16[1,384,16,128]{3,2,1,0:T(8,128)(2,1)}, bf16[1,384,16,128]{3,2,1,0:T(8,128)(2,1)}) custom-call(bf16[8,384,128]{2,1,0:T(8,128)(2,1)} %get-tuple-element.68.refs_0_, bf16[8,384,128]{2,1,0:T(8,128)(2,1)} %get-tuple-element.71.refs_1_, bf16[8,384,128]{2,1,0:T(8,128)(2,1)} %get-tuple-element.72.refs_2_, ...), custom_call_target="tpu_custom_call" | custom-call | tf_op jit(solution)/shard_map/to_tokens/pallas_call | solution.py:208
  124.4 5.7 %premerge.1 = (bf16[1,384,16,128]{3,2,1,0:T(8,128)(2,1)}, bf16[1,384,16,128]{3,2,1,0:T(8,128)(2,1)}) custom-call(s32[2]{0:T(128)} %pad_add_fusion.even, bf16[8,2,384,128]{3,2,1,0:T(8,128)(2,1)} %get-tuple-element.76.refs_0_, bf16[8,2,384,128]{3,2,1,0:T(8,128)(2,1)} %get-tuple-element.77.refs_1_, bf16[8,2,128,128]{3,2,1,0:T(8,128)(2,1)} %copy-done.5, ...), custom_call_target="tpu_custom_call" | custom-call | tf_op jit(solution)/shard_map/premerge/pallas_call | solution.py:280
  130.1 1.7 %collective-permute-done.19.from_a = bf16[64,2,16,128]{3,2,1,0:T(8,128)(2,1)S(1)} collective-permute-done((bf16[64,2,16,128]{3,2,1,0:T(8,128)(2,1)}, bf16[64,2,16,128]{3,2,1,0:T(8,128)(2,1)S(1)}, u32[]{:S(2)}, u32[]{:S(2)}) %collective-permute-start.19) | collective-permute-done | bytes 524320 | tf_op jit(solution)/shard_map/ppermute | solution.py:60
  131.8 0.8 copy-done.11
  132.6 0.2 copy-done.12
  132.8 3.2 %finish.1 = (bf16[1,384,16,128]{3,2,1,0:T(8,128)(2,1)}, bf16[1,384,16,128]{3,2,1,0:T(8,128)(2,1)}) custom-call(s32[2]{0:T(128)} %pad_add_fusion.even, bf16[1,384,16,128]{3,2,1,0:T(8,128)(2,1)} %get-tuple-element.82.dk, bf16[1,384,16,128]{3,2,1,0:T(8,128)(2,1)} %get-tuple-element.83.dv, ...), custom_call_target="tpu_custom_call", output_to_operand_aliasing={{0}: (1, {}), {1}: (2, {})} | custom-call | tf_op jit(solution)/shard_map/finish/pallas_call | solution.py:303
  (44 shorter events, 0.2 us)
Async XLA Ops:
  1.4 5.7 %collective-permute-start.2 = (bf16[4,2,16,128]{3,2,1,0:T(8,128)(2,1)S(1)}, bf16[4,2,16,128]{3,2,1,0:T(8,128)(2,1)S(1)}, u32[]{:S(2)}, u32[]{:S(2)}) collective-permute-start(bf16[4,2,16,128]{3,2,1,0:T(8,128)(2,1)S(1)} %pad_maximum_fusion.4), channel_id=1, source_target_pairs={{0,24},{2,26},{4,28},{6,30},{8,16},{10,18},{12,20},{14,22},{16,8},... | collective-permute-start | bytes 98312 | tf_op jit(solution)/shard_map/ppermute | solution.py:68
  3.6 5.4 %collective-permute-start.1 = (bf16[4,2,16,128]{3,2,1,0:T(8,128)(2,1)S(1)}, bf16[4,2,16,128]{3,2,1,0:T(8,128)(2,1)S(1)}, u32[]{:S(2)}, u32[]{:S(2)}) collective-permute-start(bf16[4,2,16,128]{3,2,1,0:T(8,128)(2,1)S(1)} %pad_maximum_fusion.4), channel_id=1, source_target_pairs={{0,16},{2,18},{4,20},{6,22},{8,24},{10,26},{12,28},{14,30},{16,0},... | collective-permute-start | bytes 98312 | tf_op jit(solution)/shard_map/ppermute | solution.py:68
  4.3 4.7 %collective-permute-start = (bf16[4,2,16,128]{3,2,1,0:T(8,128)(2,1)S(1)}, bf16[4,2,16,128]{3,2,1,0:T(8,128)(2,1)S(1)}, u32[]{:S(2)}, u32[]{:S(2)}) collective-permute-start(bf16[4,2,16,128]{3,2,1,0:T(8,128)(2,1)S(1)} %pad_maximum_fusion.4), channel_id=1, source_target_pairs={{0,8},{2,10},{4,12},{6,14},{8,0},{10,2},{12,4},{14,6},{16,24},{18,... | collective-permute-start | bytes 98312 | tf_op jit(solution)/shard_map/ppermute | solution.py:68
  7.0 2.1 %copy-start.16 = (bf16[1,4,16,128]{3,2,1,0:T(8,128)(2,1)S(1)}, bf16[1,4,16,128]{3,2,1,0:T(8,128)(2,1)}, u32[]{:S(2)}) copy-start(bf16[1,4,16,128]{3,2,1,0:T(8,128)(2,1)} %param.10) | copy-start | bytes 49156
  7.0 2.0 %copy-start.17 = (bf16[1,4,16,128]{3,2,1,0:T(8,128)(2,1)S(1)}, bf16[1,4,16,128]{3,2,1,0:T(8,128)(2,1)}, u32[]{:S(2)}) copy-start(bf16[1,4,16,128]{3,2,1,0:T(8,128)(2,1)} %param.9) | copy-start | bytes 49156
  9.0 11.5 %collective-permute-start.7 = (bf16[16,2,16,128]{3,2,1,0:T(8,128)(2,1)S(1)}, bf16[16,2,16,128]{3,2,1,0:T(8,128)(2,1)S(1)}, u32[]{:S(2)}, u32[]{:S(2)}) collective-permute-start(bf16[16,2,16,128]{3,2,1,0:T(8,128)(2,1)S(1)} %pad_maximum_fusion.3), channel_id=1, source_target_pairs={{0,96},{2,98},{4,100},{6,102},{8,104},{10,106},{12,108},{14,110},{... | collective-permute-start | bytes 393224 | tf_op jit(solution)/shard_map/ppermute | solution.py:68
  12.9 9.2 %collective-permute-start.6 = (bf16[16,2,16,128]{3,2,1,0:T(8,128)(2,1)S(1)}, bf16[16,2,16,128]{3,2,1,0:T(8,128)(2,1)S(1)}, u32[]{:S(2)}, u32[]{:S(2)}) collective-permute-start(bf16[16,2,16,128]{3,2,1,0:T(8,128)(2,1)S(1)} %pad_maximum_fusion.3), channel_id=1, source_target_pairs={{0,64},{2,66},{4,68},{6,70},{8,72},{10,74},{12,76},{14,78},{16,80}... | collective-permute-start | bytes 393224 | tf_op jit(solution)/shard_map/ppermute | solution.py:68
  12.9 9.4 %collective-permute-start.5 = (bf16[16,2,16,128]{3,2,1,0:T(8,128)(2,1)S(1)}, bf16[16,2,16,128]{3,2,1,0:T(8,128)(2,1)S(1)}, u32[]{:S(2)}, u32[]{:S(2)}) collective-permute-start(bf16[16,2,16,128]{3,2,1,0:T(8,128)(2,1)S(1)} %pad_maximum_fusion.3), channel_id=1, source_target_pairs={{0,32},{2,34},{4,36},{6,38},{8,40},{10,42},{12,44},{14,46},{16,48}... | collective-permute-start | bytes 393224 | tf_op jit(solution)/shard_map/ppermute | solution.py:68
  13.6 24.5 %collective-permute-start.3 = (bf16[64,2,16,128]{3,2,1,0:T(8,128)(2,1)S(1)}, bf16[64,2,16,128]{3,2,1,0:T(8,128)(2,1)S(1)}, u32[]{:S(2)}, u32[]{:S(2)}) collective-permute-start(bf16[64,2,16,128]{3,2,1,0:T(8,128)(2,1)S(1)} %pad_maximum_fusion), channel_id=1, source_target_pairs={{0,16},{2,18},{4,20},{6,22},{8,24},{10,26},{12,28},{14,30},{16,0},... | collective-permute-start | bytes 1572872 | tf_op jit(solution)/shard_map/ppermute | solution.py:60
  15.5 22.6 %collective-permute-start.4 = (bf16[64,2,16,128]{3,2,1,0:T(8,128)(2,1)S(1)}, bf16[64,2,16,128]{3,2,1,0:T(8,128)(2,1)S(1)}, u32[]{:S(2)}, u32[]{:S(2)}) collective-permute-start(bf16[64,2,16,128]{3,2,1,0:T(8,128)(2,1)S(1)} %pad_maximum_fusion.1), channel_id=1, source_target_pairs={{0,0},{2,2},{4,4},{6,6},{8,8},{10,10},{12,12},{14,14},{16,32},{18,... | collective-permute-start | bytes 1572872 | tf_op jit(solution)/shard_map/ppermute | solution.py:60
  22.4 10.1 %copy-start = (bf16[64,2,16,128]{3,2,1,0:T(8,128)(2,1)}, bf16[64,2,16,128]{3,2,1,0:T(8,128)(2,1)S(1)}, u32[]{:S(2)}) copy-start(bf16[64,2,16,128]{3,2,1,0:T(8,128)(2,1)S(1)} %pad_maximum_fusion.2.refs_0_) | copy-start | bytes 1572868
  22.4 26.6 %collective-permute-start.10 = (bf16[64,2,16,128]{3,2,1,0:T(8,128)(2,1)S(1)}, bf16[64,2,16,128]{3,2,1,0:T(8,128)(2,1)S(1)}, u32[]{:S(2)}, u32[]{:S(2)}) collective-permute-start(bf16[64,2,16,128]{3,2,1,0:T(8,128)(2,1)S(1)} %pad_maximum_fusion.2.refs_0_), channel_id=1, source_target_pairs={{0,6},{2,4},{4,2},{6,0},{8,14},{10,12},{12,10},{14,8},{16,22},{18,... | collective-permute-start | bytes 1572872 | tf_op jit(solution)/shard_map/ppermute | solution.py:68
  25.5 24.0 %collective-permute-start.9 = (bf16[64,2,16,128]{3,2,1,0:T(8,128)(2,1)S(1)}, bf16[64,2,16,128]{3,2,1,0:T(8,128)(2,1)S(1)}, u32[]{:S(2)}, u32[]{:S(2)}) collective-permute-start(bf16[64,2,16,128]{3,2,1,0:T(8,128)(2,1)S(1)} %pad_maximum_fusion.2.refs_0_), channel_id=1, source_target_pairs={{0,4},{2,6},{4,0},{6,2},{8,12},{10,14},{12,8},{14,10},{16,20},{18,... | collective-permute-start | bytes 1572872 | tf_op jit(solution)/shard_map/ppermute | solution.py:68
  27.2 28.1 %collective-permute-start.8 = (bf16[64,2,16,128]{3,2,1,0:T(8,128)(2,1)S(1)}, bf16[64,2,16,128]{3,2,1,0:T(8,128)(2,1)S(1)}, u32[]{:S(2)}, u32[]{:S(2)}) collective-permute-start(bf16[64,2,16,128]{3,2,1,0:T(8,128)(2,1)S(1)} %pad_maximum_fusion.2.refs_0_), channel_id=1, source_target_pairs={{0,2},{2,0},{4,6},{6,4},{8,10},{10,8},{12,14},{14,12},{16,18},{18,... | collective-permute-start | bytes 1572872 | tf_op jit(solution)/shard_map/ppermute | solution.py:68
  38.1 0.8 copy-start.1
  38.1 0.9 copy-start.2
  43.1 18.8 %collective-permute-start.13 = (bf16[128,2,8,128]{3,2,1,0:T(8,128)(2,1)}, bf16[128,2,8,128]{3,2,1,0:T(8,128)(2,1)S(1)}, u32[]{:S(2)}, u32[]{:S(2)}) collective-permute-start(bf16[128,2,8,128]{3,2,1,0:T(8,128)(2,1)} %get-tuple-element.69), channel_id=1, source_target_pairs={{0,2},{2,0},{4,6},{6,4},{8,10},{10,8},{12,14},{14,12},{16,18},{18,... | collective-permute-start | bytes 1572872 | tf_op jit(solution)/shard_map/ppermute | solution.py:60
  44.7 19.1 %collective-permute-start.14 = (bf16[128,2,8,128]{3,2,1,0:T(8,128)(2,1)}, bf16[128,2,8,128]{3,2,1,0:T(8,128)(2,1)S(1)}, u32[]{:S(2)}, u32[]{:S(2)}) collective-permute-start(bf16[128,2,8,128]{3,2,1,0:T(8,128)(2,1)} %get-tuple-element.70), channel_id=1, source_target_pairs={{0,0},{2,4},{4,2},{6,8},{8,6},{10,12},{12,10},{14,14},{16,16},{18,... | collective-permute-start | bytes 1572872 | tf_op jit(solution)/shard_map/ppermute | solution.py:60
  49.1 6.3 %copy-start.13 = (bf16[64,2,16,128]{3,2,1,0:T(8,128)(2,1)}, bf16[64,2,16,128]{3,2,1,0:T(8,128)(2,1)S(1)}, u32[]{:S(2)}) copy-start(bf16[64,2,16,128]{3,2,1,0:T(8,128)(2,1)S(1)} %collective-permute-done.10.refs_3_) | copy-start | bytes 1572868
  49.1 31.9 %collective-permute-start.11 = (bf16[128,2,8,128]{3,2,1,0:T(8,128)(2,1)}, bf16[128,2,8,128]{3,2,1,0:T(8,128)(2,1)S(1)}, u32[]{:S(2)}, u32[]{:S(2)}) collective-permute-start(bf16[128,2,8,128]{3,2,1,0:T(8,128)(2,1)} %get-tuple-element.65), channel_id=1, source_target_pairs={{0,2},{2,0},{4,6},{6,4},{8,10},{10,8},{12,14},{14,12},{16,18},{18,... | collective-permute-start | bytes 1572872 | tf_op jit(solution)/shard_map/ppermute | solution.py:60
  49.6 5.8 %copy-start.14 = (bf16[64,2,16,128]{3,2,1,0:T(8,128)(2,1)}, bf16[64,2,16,128]{3,2,1,0:T(8,128)(2,1)S(1)}, u32[]{:S(2)}) copy-start(bf16[64,2,16,128]{3,2,1,0:T(8,128)(2,1)S(1)} %collective-permute-done.9.refs_2_) | copy-start | bytes 1572868
  49.6 31.4 %collective-permute-start.12 = (bf16[128,2,8,128]{3,2,1,0:T(8,128)(2,1)}, bf16[128,2,8,128]{3,2,1,0:T(8,128)(2,1)S(1)}, u32[]{:S(2)}, u32[]{:S(2)}) collective-permute-start(bf16[128,2,8,128]{3,2,1,0:T(8,128)(2,1)} %get-tuple-element.66), channel_id=1, source_target_pairs={{0,0},{2,4},{4,2},{6,8},{8,6},{10,12},{12,10},{14,14},{16,16},{18,... | collective-permute-start | bytes 1572872 | tf_op jit(solution)/shard_map/ppermute | solution.py:60
  55.4 0.8 copy-start.15
  61.9 1.8 %copy-start.9 = (bf16[128,2,8,128]{3,2,1,0:T(8,128)(2,1)}, bf16[128,2,8,128]{3,2,1,0:T(8,128)(2,1)S(1)}, u32[]{:S(2)}) copy-start(bf16[128,2,8,128]{3,2,1,0:T(8,128)(2,1)S(1)} %collective-permute-done.13.sa) | copy-start | bytes 1572868
  63.8 0.9 copy-start.10
  76.5 21.9 %collective-permute-start.16 = (bf16[8,2,128,128]{3,2,1,0:T(8,128)(2,1)}, bf16[8,2,128,128]{3,2,1,0:T(8,128)(2,1)S(1)}, u32[]{:S(2)}, u32[]{:S(2)}) collective-permute-start(bf16[8,2,128,128]{3,2,1,0:T(8,128)(2,1)} %get-tuple-element.79), channel_id=1, source_target_pairs={{0,2},{2,0},{4,6},{6,4},{8,10},{10,8},{12,14},{14,12},{16,18},{18,... | collective-permute-start | bytes 1572872 | tf_op jit(solution)/shard_map/ppermute | solution.py:60
  76.6 21.8 %collective-permute-start.18 = (bf16[8,2,128,128]{3,2,1,0:T(8,128)(2,1)}, bf16[8,2,128,128]{3,2,1,0:T(8,128)(2,1)S(1)}, u32[]{:S(2)}, u32[]{:S(2)}) collective-permute-start(bf16[8,2,128,128]{3,2,1,0:T(8,128)(2,1)} %get-tuple-element.81), channel_id=1, source_target_pairs={{0,0},{2,4},{4,2},{6,8},{8,6},{10,12},{12,10},{14,14},{16,16},{18,... | collective-permute-start | bytes 1572872 | tf_op jit(solution)/shard_map/ppermute | solution.py:60
  81.0 0.8 copy-start.7
  81.8 0.8 copy-start.8
  94.4 9.5 %collective-permute-start.15 = (bf16[8,2,128,128]{3,2,1,0:T(8,128)(2,1)}, bf16[8,2,128,128]{3,2,1,0:T(8,128)(2,1)S(1)}, u32[]{:S(2)}, u32[]{:S(2)}) collective-permute-start(bf16[8,2,128,128]{3,2,1,0:T(8,128)(2,1)} %get-tuple-element.78), channel_id=1, source_target_pairs={{0,2},{2,0},{4,6},{6,4},{8,10},{10,8},{12,14},{14,12},{16,18},{18,... | collective-permute-start | bytes 1572872 | tf_op jit(solution)/shard_map/ppermute | solution.py:60
  94.8 13.4 %collective-permute-start.17 = (bf16[8,2,128,128]{3,2,1,0:T(8,128)(2,1)}, bf16[8,2,128,128]{3,2,1,0:T(8,128)(2,1)S(1)}, u32[]{:S(2)}, u32[]{:S(2)}) collective-permute-start(bf16[8,2,128,128]{3,2,1,0:T(8,128)(2,1)} %get-tuple-element.80), channel_id=1, source_target_pairs={{0,0},{2,4},{4,2},{6,8},{8,6},{10,12},{12,10},{14,14},{16,16},{18,... | collective-permute-start | bytes 1572872 | tf_op jit(solution)/shard_map/ppermute | solution.py:60
  98.5 9.8 %copy-start.3 = (bf16[8,2,128,128]{3,2,1,0:T(8,128)(2,1)}, bf16[8,2,128,128]{3,2,1,0:T(8,128)(2,1)S(1)}, u32[]{:S(2)}) copy-start(bf16[8,2,128,128]{3,2,1,0:T(8,128)(2,1)S(1)} %collective-permute-done.16.refs_3_.refs_5_) | copy-start | bytes 1572868
  98.5 9.7 %copy-start.4 = (bf16[8,2,128,128]{3,2,1,0:T(8,128)(2,1)}, bf16[8,2,128,128]{3,2,1,0:T(8,128)(2,1)S(1)}, u32[]{:S(2)}) copy-start(bf16[8,2,128,128]{3,2,1,0:T(8,128)(2,1)S(1)} %collective-permute-done.18.refs_5_.refs_7_) | copy-start | bytes 1572868
  103.9 4.3 %copy-start.5 = (bf16[8,2,128,128]{3,2,1,0:T(8,128)(2,1)}, bf16[8,2,128,128]{3,2,1,0:T(8,128)(2,1)S(1)}, u32[]{:S(2)}) copy-start(bf16[8,2,128,128]{3,2,1,0:T(8,128)(2,1)S(1)} %collective-permute-done.15.refs_2_.refs_4_) | copy-start | bytes 1572868
  108.2 0.8 copy-start.6
  112.2 19.5 %collective-permute-start.19 = (bf16[64,2,16,128]{3,2,1,0:T(8,128)(2,1)}, bf16[64,2,16,128]{3,2,1,0:T(8,128)(2,1)S(1)}, u32[]{:S(2)}, u32[]{:S(2)}) collective-permute-start(bf16[64,2,16,128]{3,2,1,0:T(8,128)(2,1)} %get-tuple-element.88), channel_id=1, source_target_pairs={{0,16},{2,18},{4,20},{6,22},{8,24},{10,26},{12,28},{14,30},{16,0},... | collective-permute-start | bytes 1572872 | tf_op jit(solution)/shard_map/ppermute | solution.py:60
  115.5 16.3 %collective-permute-start.20 = (bf16[64,2,16,128]{3,2,1,0:T(8,128)(2,1)}, bf16[64,2,16,128]{3,2,1,0:T(8,128)(2,1)S(1)}, u32[]{:S(2)}, u32[]{:S(2)}) collective-permute-start(bf16[64,2,16,128]{3,2,1,0:T(8,128)(2,1)} %get-tuple-element.89), channel_id=1, source_target_pairs={{0,0},{2,2},{4,4},{6,6},{8,8},{10,10},{12,12},{14,14},{16,32},{18,... | collective-permute-start | bytes 1572872 | tf_op jit(solution)/shard_map/ppermute | solution.py:60
  131.8 0.8 copy-start.11
  131.8 1.0 copy-start.12
